TPU v7x, 128 devices: a whole 4x4x4 slice. The times are simulated.
128 devices in a mesh: qrow: 8 (over y, x_lo), kcol: 16 (over z, x_hi, core).
Axes of the slice: x: 4 (x_hi: 2, x_lo: 2; x = x_hi * 2 + x_lo), y: 4, z: 4, core: 2. Of those that a mesh axis runs over, the one named last changes fastest.
Arguments:
- queries: bfloat16 [8192, 4096], P('qrow', 'kcol'), may hold values from -24 to 24
- key_states: bfloat16 [8192, 512], P(('kcol', 'qrow')), may hold values from -8 to 8
- value_states: bfloat16 [8192, 512], P(('kcol', 'qrow')), may hold values from -6 to 6
Outputs:
- mixed: bfloat16 [8192, 4096], P(('qrow', 'kcol'))
- log_sums: float32 [8192, 32], P(('qrow', 'kcol'))
All inputs are finite; a program needn't handle non-finite values.
Results may differ from a plain program's by a relative error of at most 0.0048.
Values may be sent and summed in bfloat16 or wider, within the bound.
No kernel may reach another device: no remote copies, remote signals or barrier semaphores. Data moves between devices by JAX's collectives and lax.ppermute only.
A program may use at most 128 MiB of HBM per device.

v0:
```python
import math

import jax
import jax.numpy as jnp
from jax import lax
from jax.sharding import PartitionSpec as P

HQ = 32
KVH = 4
HD = 128
GROUP = 8


NEG_FILL = -1e30


def joined(part, axis, combine):
    gathered = jax.tree.map(lambda a: lax.all_gather(a, axis), part)

    def take(source):
        return jax.tree.map(lambda a: lax.dynamic_index_in_dim(a, source, 0, False), gathered)

    return lax.fori_loop(
        1, lax.axis_size(axis), lambda source, state: combine(state, take(source)), take(0)
    )


def group_partial(query_group, positions, keys_group, values_group, key_pos):
    score_scale = 1.0 / math.sqrt(query_group.shape[-1])
    scores = (
        jnp.einsum("rnd,kd->rnk", query_group, keys_group, preferred_element_type=jnp.float32)
        * score_scale
    )
    allowed = key_pos[None, None, :] <= positions[:, None, None]
    scores = jnp.where(allowed, scores, NEG_FILL)
    block_peak = jnp.max(scores, axis=2)
    weights = jnp.where(allowed, jnp.exp(scores - block_peak[:, :, None]), 0.0)
    block_total = jnp.sum(weights, axis=2)
    numerator = jnp.einsum(
        "rnk,kd->rnd",
        weights.astype(jnp.bfloat16),
        values_group,
        preferred_element_type=jnp.float32,
    )
    normed = (numerator / jnp.where(block_total > 0, block_total, 1.0)[:, :, None]).astype(
        jnp.bfloat16
    )
    return (block_peak, block_total, normed)


def span_partial(query_rows, positions, block_keys, block_values, key_start):
    row_total, group_count, per_group, head_width = query_rows.shape
    key_pos = key_start + jnp.arange(block_keys.shape[0], dtype=jnp.int32)

    def compute(operand):
        partials = [
            group_partial(
                query_rows[:, group_id],
                positions,
                block_keys[:, group_id],
                block_values[:, group_id],
                key_pos,
            )
            for group_id in range(group_count)
        ]
        return (
            jnp.concatenate([partial_value[0] for partial_value in partials], axis=1),
            jnp.concatenate([partial_value[1] for partial_value in partials], axis=1),
            jnp.concatenate([partial_value[2] for partial_value in partials], axis=1),
        )

    def skipped(operand):
        head_count = group_count * per_group
        return (
            jnp.full((row_total, head_count), NEG_FILL, jnp.float32),
            jnp.zeros((row_total, head_count), jnp.float32),
            jnp.zeros((row_total, head_count, head_width), jnp.bfloat16),
        )

    return lax.cond(jnp.max(positions) < key_start, skipped, compute, 0)


def combine_totals(first_pair, second_pair):
    joint_top = jnp.maximum(first_pair[0], second_pair[0])
    joint_total = first_pair[1] * jnp.exp(first_pair[0] - joint_top) + second_pair[1] * jnp.exp(
        second_pair[0] - joint_top
    )
    return (joint_top, joint_total)


def per_device(queries, key_states, value_states):
    row_count = lax.axis_size("qrow")
    col_count = lax.axis_size("kcol")
    row_index = lax.axis_index("qrow")
    col_index = lax.axis_index("kcol")
    span_rows = queries.shape[0]
    half_rows = span_rows // 2
    shard_rows = key_states.shape[0]
    block_len = shard_rows * row_count
    positions = row_index * span_rows + jnp.arange(span_rows, dtype=jnp.int32)
    full_queries = lax.all_gather(queries, "kcol", axis=1, tiled=True)
    block_keys, block_values = (
        lax.all_gather(key_states, "qrow", axis=0, tiled=True),
        lax.all_gather(value_states, "qrow", axis=0, tiled=True),
    )
    grouped = full_queries.reshape(span_rows, KVH, GROUP, HD)
    block_keys = block_keys.reshape(block_len, KVH, HD)
    block_values = block_values.reshape(block_len, KVH, HD)
    key_start = col_index * block_len
    halves = [
        span_partial(
            grouped[half_id * half_rows : (half_id + 1) * half_rows],
            positions[half_id * half_rows : (half_id + 1) * half_rows],
            block_keys,
            block_values,
            key_start,
        )
        for half_id in range(2)
    ]
    block_peak = jnp.concatenate([halves[0][0], halves[1][0]], axis=0)
    block_total = jnp.concatenate([halves[0][1], halves[1][1]], axis=0)
    normed = jnp.concatenate([halves[0][2], halves[1][2]], axis=0)
    run_top, run_total = joined((block_peak, block_total), "kcol", combine_totals)
    share = block_total * jnp.exp(block_peak - run_top) / run_total
    terms = (normed.astype(jnp.float32) * share[:, :, None]).reshape(span_rows, HQ * HD)
    mixed_rows = lax.psum_scatter(terms, "kcol", scatter_dimension=0, tiled=True).astype(
        jnp.bfloat16
    )
    piece_rows = span_rows // col_count
    log_sums = lax.dynamic_slice_in_dim(
        run_top + jnp.log(run_total), col_index * piece_rows, piece_rows, 0
    )
    return (mixed_rows, log_sums)


def solution(mesh):
    placed = (P("qrow", "kcol"), P(("kcol", "qrow"), None), P(("kcol", "qrow"), None))
    return jax.shard_map(
        per_device,
        mesh=mesh,
        in_specs=placed,
        out_specs=(P(("qrow", "kcol"), None), P(("qrow", "kcol"), None)),
        check_vma=False,
    )
```

profile of v0, /device:TPU:2, one launch (start us, length us, event | category | flops | bytes accessed | tf_op | source)
XLA Modules:
  0.0 523.5 jit_solution(8717411647197930278)
XLA Ops:
  9.3 31.2 %all_gather.22 = bf16[512,512]{1,0:T(8,128)(2,1)S(1)} all-gather(bf16[64,512]{1,0:T(8,128)(2,1)} %param.10), channel_id=1, replica_groups=mesh['qrow'=8,'kcol'=16] {'qrow'}, dimensions={0}, use_global_device_ids=true | all-gather | bytes 589824 | tf_op jit(solution)/shard_map/all_gather | solution.py:103
  40.8 32.6 %all_gather.23 = bf16[512,512]{1,0:T(8,128)(2,1)S(1)} all-gather(bf16[64,512]{1,0:T(8,128)(2,1)} %param.11), channel_id=1, replica_groups=mesh['qrow'=8,'kcol'=16] {'qrow'}, dimensions={0}, use_global_device_ids=true | all-gather | bytes 589824 | tf_op jit(solution)/shard_map/all_gather | solution.py:104
  75.6 17.9 %all-gather.6.cloned.1.call-done = bf16[1024,4096]{0,1:T(8,128)(2,1)} async-done(((bf16[1024,256]{0,1:T(8,128)(2,1)}), bf16[1024,4096]{0,1:T(8,128)(2,1)}) %all-gather.6.cloned.1.call-update) | async-done | bytes 8388624 | tf_op jit(solution)/shard_map/all_gather | solution.py:101
  93.5 58.3 %conditional.2 = (f32[512,32]{0,1:T(8,128)S(1)}, f32[512,32]{0,1:T(8,128)S(1)}, bf16[512,4096]{1,0:T(8,128)(2,1)}) conditional(s32[]{:T(128)} %convert_element_type.61, (s32[512]{0:T(512)S(1)}, s32[512]{0:T(512)S(1)}, bf16[1024,4096]{0,1:T(8,128)(2,1)}, bf16[512,4,128]{0,2,1:T(8,128)(2,1)S(1)}, bf16[512,4,128]{0,2,1:T(8,128)(2,1)S(1)}) %tuple.117, ...), branch_computations={%region_1.10_spmd, %region_10.11_spmd} | conditional | flops 4414865408 | bytes 172691520 | solution.py:80
  93.8 4.4 slice.64
  98.4 6.1 %fusion = (f32[512,8]{0,1:T(8,128)S(1)}, f32[512,8,512]{0,2,1:T(8,128)}) fusion(pred[512,512]{0,1:T(8,128)(4,1)S(1)} %broadcast_compare_fusion, bf16[512,4,8,128]{0,3,2,1:T(8,128)(2,1)} %bitcast.142, bf16[512,4,128]{2,0,1:T(8,128)(2,1)S(1)} %copy.70), kind=kOutput, calls=%fused_computation.8 | convolution fusion | flops 543158272 | bytes 9846784 | tf_op jit(solution)/shard_map/cond/branch_0_fun/rnd,kd->rnk/dot_general | solution.py:31
  107.0 10.5 %fusion.5 = (f32[512,8]{0,1:T(8,128)S(1)}, f32[512,8]{0,1:T(8,128)S(1)}, f32[512,8]{0,1:T(8,128)S(1)}, f32[512,8]{0,1:T(8,128)S(1)}, f32[512,8,512]{0,2,1:T(8,128)}) fusion(f32[512,8,512]{0,2,1:T(8,128)} %get-tuple-element.241, f32[512,8]{0,1:T(8,128)S(1)} %get-tuple-element.240, pred[512,512]{0,1:T(8,128)(4,1)S(1)} %broadcast_compare_fusion, ...), kind=kOutput, calls=%fused_computation.13 | convolution fusion | flops 566214656 | bytes 35078144 | tf_op jit(solution)/shard_map/cond/branch_0_fun/rnd,kd->rnk/dot_general | solution.py:31
  117.5 5.9 %divide_convert_fusion.3 = bf16[512,8,128]{0,2,1:T(8,128)(2,1)S(1)} fusion(f32[512,8]{0,1:T(8,128)S(1)} %compare_select_fusion.3, f32[512,8,512]{0,2,1:T(8,128)} %get-tuple-element.241, f32[512,8]{0,1:T(8,128)S(1)} %get-tuple-element.240, pred[512,512]{0,1:T(8,128)(4,1)S(1)} %broadcast_compare_fusion, bf16[512,4,128]{0,2,1:T(8,128)(2,1)S(1)} %get-tuple-element.155), kind=kOutput, calls=%fused_computation.32 | convolution fusion | flops 548405248 | bytes 9863168 | tf_op jit(solution)/shard_map/cond/branch_0_fun/rnk,kd->rnd/dot_general | solution.py:39
  123.5 8.4 %fusion.7 = (f32[512,8]{0,1:T(8,128)S(1)}, f32[512,8]{0,1:T(8,128)S(1)}, f32[512,8]{0,1:T(8,128)S(1)}) fusion(f32[512,8,512]{0,2,1:T(8,128)} %get-tuple-element.242, f32[512,8]{0,1:T(8,128)S(1)} %get-tuple-element.213, pred[512,512]{0,1:T(8,128)(4,1)S(1)} %broadcast_compare_fusion, f32[512,8]{0,1:T(8,128)S(1)} %get-tuple-element.214, ...), kind=kLoop, calls=%fused_computation.15 | loop fusion | flops 31444992 | bytes 25526272 | tf_op jit(solution)/shard_map/cond/branch_0_fun/reduce_sum | solution.py:38
  131.8 5.9 %divide_convert_fusion.2 = bf16[512,8,128]{0,2,1:T(8,128)(2,1)S(1)} fusion(f32[512,8]{0,1:T(8,128)S(1)} %compare_select_fusion.2, f32[512,8,512]{0,2,1:T(8,128)} %get-tuple-element.242, f32[512,8]{0,1:T(8,128)S(1)} %get-tuple-element.213, pred[512,512]{0,1:T(8,128)(4,1)S(1)} %broadcast_compare_fusion, bf16[512,4,128]{0,2,1:T(8,128)(2,1)S(1)} %get-tuple-element.155), kind=kOutput, calls=%fused_computation.31 | convolution fusion | flops 548405248 | bytes 9863168 | tf_op jit(solution)/shard_map/cond/branch_0_fun/rnk,kd->rnd/dot_general | solution.py:39
  137.8 2.6 divide_convert_fusion.1
  140.4 2.6 divide_convert_fusion
  142.9 2.3 pad_maximum_fusion
  145.2 6.4 %copy.93 = bf16[512,4096]{1,0:T(8,128)(2,1)} copy(bf16[512,4096]{0,1:T(8,128)(2,1)} %bitcast.138) | data formatting | bytes 8388608 | tf_op jit(solution)/shard_map/cond | solution.py:80
  151.9 58.6 %conditional.3 = (f32[512,32]{0,1:T(8,128)S(1)}, f32[512,32]{0,1:T(8,128)S(1)}, bf16[512,4096]{1,0:T(8,128)(2,1)}) conditional(s32[]{:T(128)} %convert_element_type.62, (s32[512]{0:T(512)S(1)}, s32[512]{0:T(512)S(1)}, bf16[1024,4096]{0,1:T(8,128)(2,1)}, bf16[512,4,128]{0,2,1:T(8,128)(2,1)S(1)}, bf16[512,4,128]{0,2,1:T(8,128)(2,1)S(1)}) %tuple.118, ...), branch_computations={%region_12.21_spmd, %region_21.22_spmd} | conditional | flops 4414865408 | bytes 172691520 | solution.py:80
  152.1 4.4 slice.78
  156.8 6.1 %fusion.56 = (f32[512,8]{0,1:T(8,128)S(1)}, f32[512,8,512]{0,2,1:T(8,128)}) fusion(pred[512,512]{0,1:T(8,128)(4,1)S(1)} %broadcast_compare_fusion.1, bf16[512,4,8,128]{0,3,2,1:T(8,128)(2,1)} %bitcast.146, bf16[512,4,128]{2,0,1:T(8,128)(2,1)S(1)} %copy.71), kind=kOutput, calls=%fused_computation.80 | convolution fusion | flops 543158272 | bytes 9846784 | tf_op jit(solution)/shard_map/cond/branch_0_fun/rnd,kd->rnk/dot_general | solution.py:31
  165.4 10.7 %fusion.61 = (f32[512,8]{0,1:T(8,128)S(1)}, f32[512,8]{0,1:T(8,128)S(1)}, f32[512,8]{0,1:T(8,128)S(1)}, f32[512,8]{0,1:T(8,128)S(1)}, f32[512,8,512]{0,2,1:T(8,128)}) fusion(f32[512,8,512]{0,2,1:T(8,128)} %get-tuple-element.248, f32[512,8]{0,1:T(8,128)S(1)} %get-tuple-element.247, pred[512,512]{0,1:T(8,128)(4,1)S(1)} %broadcast_compare_fusion.1, ...), kind=kOutput, calls=%fused_computation.85 | convolution fusion | flops 566214656 | bytes 35078144 | tf_op jit(solution)/shard_map/cond/branch_0_fun/rnd,kd->rnk/dot_general | solution.py:31
  176.1 5.9 %divide_convert_fusion.7 = bf16[512,8,128]{0,2,1:T(8,128)(2,1)S(1)} fusion(f32[512,8]{0,1:T(8,128)S(1)} %compare_select_fusion.7, f32[512,8,512]{0,2,1:T(8,128)} %get-tuple-element.248, f32[512,8]{0,1:T(8,128)S(1)} %get-tuple-element.247, pred[512,512]{0,1:T(8,128)(4,1)S(1)} %broadcast_compare_fusion.1, bf16[512,4,128]{0,2,1:T(8,128)(2,1)S(1)} %get-tuple-element.160), kind=kOutput, calls=%fused_computation.104 | convolution fusion | flops 548405248 | bytes 9863168 | tf_op jit(solution)/shard_map/cond/branch_0_fun/rnk,kd->rnd/dot_general | solution.py:39
  182.1 8.4 %fusion.63 = (f32[512,8]{0,1:T(8,128)S(1)}, f32[512,8]{0,1:T(8,128)S(1)}, f32[512,8]{0,1:T(8,128)S(1)}) fusion(f32[512,8,512]{0,2,1:T(8,128)} %get-tuple-element.249, f32[512,8]{0,1:T(8,128)S(1)} %get-tuple-element.220, pred[512,512]{0,1:T(8,128)(4,1)S(1)} %broadcast_compare_fusion.1, f32[512,8]{0,1:T(8,128)S(1)} %get-tuple-element.221, ...), kind=kLoop, calls=%fused_computation.87 | loop fusion | flops 31444992 | bytes 25526272 | tf_op jit(solution)/shard_map/cond/branch_0_fun/reduce_sum | solution.py:38
  190.5 5.9 %divide_convert_fusion.6 = bf16[512,8,128]{0,2,1:T(8,128)(2,1)S(1)} fusion(f32[512,8]{0,1:T(8,128)S(1)} %compare_select_fusion.6, f32[512,8,512]{0,2,1:T(8,128)} %get-tuple-element.249, f32[512,8]{0,1:T(8,128)S(1)} %get-tuple-element.220, pred[512,512]{0,1:T(8,128)(4,1)S(1)} %broadcast_compare_fusion.1, bf16[512,4,128]{0,2,1:T(8,128)(2,1)S(1)} %get-tuple-element.160), kind=kOutput, calls=%fused_computation.103 | convolution fusion | flops 548405248 | bytes 9863168 | tf_op jit(solution)/shard_map/cond/branch_0_fun/rnk,kd->rnd/dot_general | solution.py:39
  196.4 2.6 divide_convert_fusion.5
  199.0 2.6 divide_convert_fusion.4
  203.9 6.4 %copy.95 = bf16[512,4096]{1,0:T(8,128)(2,1)} copy(bf16[512,4096]{0,1:T(8,128)(2,1)} %bitcast.139) | data formatting | bytes 8388608 | tf_op jit(solution)/shard_map/cond | solution.py:80
  212.0 44.6 %all-gather.10.cloned.1.call-done = f32[16384,32]{0,1:T(8,128)} async-done(((f32[1024,32]{0,1:T(8,128)}), f32[16384,32]{0,1:T(8,128)}) %all-gather.10.cloned.1.call-update) | async-done | bytes 2097168 | tf_op jit(solution)/shard_map/all_gather | solution.py:18
  257.6 48.3 %all-gather.8.cloned.1.call-done = f32[16384,32]{0,1:T(8,128)} async-done(((f32[1024,32]{0,1:T(8,128)}), f32[16384,32]{0,1:T(8,128)}) %all-gather.8.cloned.1.call-update) | async-done | bytes 2097168 | tf_op jit(solution)/shard_map/all_gather | solution.py:18
  307.2 6.3 %copy.92 = f32[16384,32]{1,0:T(8,128)} copy(f32[16384,32]{0,1:T(8,128)} %all-gather.10.cloned.1.call-done) | data formatting | bytes 4194304 | tf_op jit(solution)/shard_map/while | solution.py:23
  313.5 4.7 copy.91
  318.2 25.1 %while.17 = (s32[]{:T(128)}, f32[1024,32]{1,0:T(8,128)S(1)}, f32[1024,32]{1,0:T(8,128)S(1)}, f32[16,1024,32]{2,1,0:T(8,128)}, f32[16,1024,32]{2,1,0:T(8,128)}, /*index=5*/s32[]{:T(128)}, s32[]{:T(128)}, s32[]{:T(128)}) while((s32[]{:T(128)}, f32[1024,32]{1,0:T(8,128)S(1)}, f32[1024,32]{1,0:T(8,128)S(1)}, f32[16,1024,32]{2,1,0:T(8,128)}, ...), condition=%wide.region_23.24_spmd, body=%wide.region_22.23_spmd.sunk | while | flops 196613 | bytes 786563 | solution.py:23
  343.9 4.6 mul.70
  348.6 20.0 %bitcast_multiply_fusion.1 = f32[1024,4096]{1,0:T(8,128)} fusion(f32[128,8,32,128]{3,2,1,0:T(8,128)S(1)} %bitcast.137, bf16[512,4096]{1,0:T(8,128)(2,1)S(1)} %copy-done.1, bf16[512,4096]{1,0:T(8,128)(2,1)S(1)} %copy-done), kind=kLoop, calls=%fused_computation.149 | loop fusion | flops 20971520 | bytes 41943040 | tf_op jit(solution)/shard_map/mul | solution.py:125
  369.3 145.5 %reduce-scatter.2.cloned.1.call-done = f32[64,4096]{1,0:T(8,128)} async-done(((f32[1024,4096]{1,0:T(8,128)}), f32[64,4096]{1,0:T(8,128)}) %reduce-scatter.2.cloned.1.call-update) | async-done | bytes 1048592 | tf_op jit(solution)/shard_map/reduce_scatter | solution.py:126
  (77 shorter events, 43.6 us)
Async XLA Ops:
  7.2 86.4 %all-gather.6.cloned.1.call-start = ((), (), s32[]{:S(2)}) async-start(), calls=%async_computation.1 | async-start | bytes 8912896 | tf_op jit(solution)/shard_map/all_gather | solution.py:101
  9.3 247.2 %all-gather.10.cloned.1.call-start = ((), (), s32[]{:S(2)}) async-start(), calls=%async_computation.4 | async-start | bytes 2228224 | tf_op jit(solution)/shard_map/all_gather | solution.py:18
  98.4 6.1 %copy-start.2 = (bf16[512,4096]{0,1:T(8,128)(2,1)S(1)}, bf16[512,4096]{0,1:T(8,128)(2,1)}, u32[]{:S(2)}) copy-start(bf16[512,4096]{0,1:T(8,128)(2,1)} %slice.64) | copy-start | bytes 12582916 | tf_op jit(solution)/shard_map/cond
  156.8 6.1 %copy-start.3 = (bf16[512,4096]{0,1:T(8,128)(2,1)S(1)}, bf16[512,4096]{0,1:T(8,128)(2,1)}, u32[]{:S(2)}) copy-start(bf16[512,4096]{0,1:T(8,128)(2,1)} %slice.78) | copy-start | bytes 12582916 | tf_op jit(solution)/shard_map/cond
  210.5 0.6 copy-start.5
  211.1 94.8 %all-gather.8.cloned.1.call-start = ((), (), s32[]{:S(2)}) async-start(), calls=%async_computation.3 | async-start | bytes 2228224 | tf_op jit(solution)/shard_map/all_gather | solution.py:18
  211.2 0.7 copy-start.7
  211.9 302.8 %reduce-scatter.2.cloned.1.call-start = ((), (), s32[]{:S(2)}) async-start(), calls=%async_computation.2 | async-start | bytes 17825792 | tf_op jit(solution)/shard_map/reduce_scatter | solution.py:126
  306.0 7.5 %copy-start.4 = (f32[16384,32]{0,1:T(8,128)S(1)}, f32[16384,32]{0,1:T(8,128)}, u32[]{:S(2)}) copy-start(f32[16384,32]{0,1:T(8,128)} %all-gather.8.cloned.1.call-done) | copy-start | bytes 6291460
  318.2 25.5 %copy-start.6 = (f32[1024,32]{0,1:T(8,128)S(1)}, f32[1024,32]{0,1:T(8,128)}, u32[]{:S(2)}) copy-start(f32[1024,32]{0,1:T(8,128)} %copy-done.5) | copy-start | bytes 393220
  318.2 25.5 %copy-start.8 = (f32[1024,32]{0,1:T(8,128)S(1)}, f32[1024,32]{0,1:T(8,128)}, u32[]{:S(2)}) copy-start(f32[1024,32]{0,1:T(8,128)} %copy-done.7) | copy-start | bytes 393220
  343.9 4.6 copy-start
  343.9 4.6 copy-start.1
Sparse Core Ops, SparseCore 0:
  11.0 82.4 all-gather.5
  211.3 45.1 all-gather.9
  259.5 46.3 all-gather.7
  368.7 145.9 reduce-scatter.1
where the time goes:
time: 530 us; the launch traced here: 524 us
  waiting for transfers between devices  256 us (48%)
  matrix products  72.4 us (14%)
  other arithmetic  70.2 us (13%)
  blocking collectives  63.8 us (12%)
  local copies, waits for them, and re-layouts  44.4 us (8%)
  between operations  15.5 us (3%)
    reduce_scatter x1, waiting for transfers between devices, per_device(): lax.psum_scatter(terms, 'kcol', scatter_dimension=0, tiled=True)  145 us
    all_gather x2, waiting for transfers between devices, joined(): gathered = jax.tree.map(lambda a: lax.all_gather(a, axis), part)  92.9 us
    dot_general x8, matrix products, group_partial(): jnp.einsum('rnd,kd->rnk', query_group, keys_group, preferred_element_type...  38.3 us
    dot_general x8, matrix products, group_partial(): jnp.einsum('rnk,kd->rnd', weights.astype(jnp.bfloat16), values_group, pre...  34 us
    all_gather x1, blocking collectives, per_device(): lax.all_gather(value_states, 'qrow', axis=0, tiled=True)  32.6 us
    all_gather x1, blocking collectives, per_device(): lax.all_gather(key_states, 'qrow', axis=0, tiled=True)  31.2 us
    add x15, other arithmetic, combine_totals(): first_pair[1] * jnp.exp(first_pair[0] - joint_top)  24.9 us
    mul x1, other arithmetic, per_device(): normed.astype(jnp.float32) * share[:, :, None]  20 us
  transfers between devices with their start and end apart: 4, of which 4 were waited for; matrix products, arithmetic and copies ran while one was open for 1% of the time, Pallas kernels for 0%

commit v1 on v0

v1 whole, which is shorter than its diff:
```python
import math

import jax
import jax.numpy as jnp
from jax import lax
from jax.experimental import pallas as pl
from jax.experimental.pallas import tpu as pltpu
from jax.sharding import PartitionSpec as P

HQ = 32
KVH = 4
HD = 128
GROUP = 8
EVERY = ("qrow", "kcol")
SPANS = 8
SLOTS = 4
SIDES = 4

NEG_FILL = -1e30
LOG2E = math.log2(math.e)
LN2 = math.log(2.0)
WIDE = GROUP * HD + HD


def device_at(span, side, slot):
    return span * 16 + side * 4 + slot


COUPLES = [(low, SPANS - 1 - low) for low in range(SPANS // 2)]
KEY_GROUPS = [
    [
        device_at(half * 4 + near, side, xh * 2 + core)
        for side in range(SIDES)
        for xh in range(2)
        for near in range(4)
    ]
    for half in range(2)
    for core in range(2)
]
QUERY_GROUPS = [
    [device_at(span, side, slot) for span in couple for slot in range(SLOTS)]
    for couple in COUPLES
    for side in range(SIDES)
]
OUTPUT_GROUPS = [
    [device_at(span, side, slot) for span in couple for side in range(SIDES)]
    for couple in COUPLES
    for slot in range(SLOTS)
]


def attend_body(info, q_ref, first_ref, second_ref, o_ref, q_two, keys, values, acc, top):
    core, half, slot = info[2], info[3], info[4]
    tile_keys = first_ref.shape[1]
    for part, ref in enumerate((first_ref, second_ref)):
        held = slice(part * tile_keys, (part + 1) * tile_keys)
        for block in range(ref.shape[0]):
            keys[block, held, :HD] = ref[block, :, :HD]
            keys[block, held, HD:] = ref[block, :, :HD]
            values[block, held, :HD] = ref[block, :, HD:]
            values[block, held, HD:] = jnp.ones((tile_keys, HD), jnp.bfloat16)

    def step(block, tile, keep):
        rows = slice(tile * 512, (tile + 1) * 512)
        scores = lax.dot_general(
            q_two[rows, :],
            keys[block],
            (((1,), (1,)), ((), ())),
            preferred_element_type=jnp.float32,
        )
        if keep is not None:
            scores = jnp.where(keep, scores, NEG_FILL)
        old = top[rows, :]
        new = jnp.maximum(old, jnp.max(scores, axis=1, keepdims=True))
        weights = jnp.exp2(scores - new[:, 0:1])
        if keep is not None:
            weights = jnp.where(keep, weights, 0.0)
        scale = jnp.exp2(old - new)
        fresh = jnp.dot(
            weights.astype(jnp.bfloat16), values[block], preferred_element_type=jnp.float32
        )
        acc[rows, :HD] = acc[rows, :HD] * scale + fresh[:, :HD]
        acc[rows, HD:] = acc[rows, HD:] * scale + fresh[:, HD:]
        top[rows, :] = new

    lane = lax.broadcasted_iota(jnp.int32, (64, HD), 1)
    for member in range(2):
        span = info[member]
        for tile in range(4):
            for head in range(GROUP):
                piece = q_ref[
                    member * SLOTS + head // 2,
                    tile * 64 : (tile + 1) * 64,
                    (head % 2) * HD : (head % 2 + 1) * HD,
                ].astype(jnp.float32) * (LOG2E / math.sqrt(HD))
                coarse = piece.astype(jnp.bfloat16)
                at = tile * 512 + head * 64
                q_two[at : at + 64, :HD] = coarse
                q_two[at : at + 64, HD:] = (piece - coarse.astype(jnp.float32)).astype(
                    jnp.bfloat16
                )
        acc[...] = jnp.zeros_like(acc)
        top[...] = jnp.full_like(top, NEG_FILL)

        @pl.loop(0, span)
        def _(block):
            for tile in range(4):
                step(block, tile, None)

        row = lax.broadcasted_iota(jnp.int32, (512, 512), 0)
        col = lax.broadcasted_iota(jnp.int32, (512, 512), 1)
        key_at = half * 256 + jnp.where(
            col < 256, core * 512 + col, (1 - core) * 512 + col - 256
        )
        for tile in range(4):
            step(span, tile, key_at <= tile * 256 + slot * 64 + row % 64)
        for tile in range(4):
            stat = jnp.zeros((64, HD), jnp.float32)
            for head in range(GROUP):
                rows = slice(tile * 512 + head * 64, tile * 512 + head * 64 + 64)
                total = acc[rows, HD:]
                some = total > 0
                safe = jnp.where(some, total, 1.0)
                o_ref[member * 4 + tile, :, head * HD : (head + 1) * HD] = (
                    acc[rows, :HD] / safe
                ).astype(jnp.bfloat16)
                log_sum = jnp.where(some, (top[rows, :] + jnp.log2(safe)) * LN2, NEG_FILL)
                stat = jnp.where(lane % GROUP == head, log_sum, stat)
            coarse = stat.astype(jnp.bfloat16).astype(jnp.float32)
            middle = (stat - coarse).astype(jnp.bfloat16).astype(jnp.float32)
            fine = stat - coarse - middle
            o_ref[member * 4 + tile, :, GROUP * HD :] = jnp.where(
                lane < 32, coarse, jnp.where(lane < 64, middle, fine)
            ).astype(jnp.bfloat16)


def attend(info, q_pieces, first, second):
    whole = pl.BlockSpec(memory_space=pltpu.VMEM)
    return pl.pallas_call(
        attend_body,
        out_shape=jax.ShapeDtypeStruct((8, 64, WIDE), jnp.bfloat16),
        in_specs=[pl.BlockSpec(memory_space=pltpu.SMEM), whole, whole, whole],
        out_specs=whole,
        scratch_shapes=[
            pltpu.VMEM((2048, 2 * HD), jnp.bfloat16),
            pltpu.VMEM((8, 512, 2 * HD), jnp.bfloat16),
            pltpu.VMEM((8, 512, 2 * HD), jnp.bfloat16),
            pltpu.VMEM((2048, 2 * HD), jnp.float32),
            pltpu.VMEM((2048, HD), jnp.float32),
        ],
        compiler_params=pltpu.CompilerParams(vmem_limit_bytes=48 * 2**20),
        cost_estimate=pl.CostEstimate(
            flops=36 * 4 * 512 * 512 * HD,
            bytes_accessed=4 * 2**20,
            transcendentals=36 * 512 * 512,
        ),
        name="attend",
    )(info, q_pieces, first, second)


def merge_body(got_ref, mixed_ref, log_ref):
    lane = lax.broadcasted_iota(jnp.int32, (64, HD), 1)
    logs = jnp.zeros((64, HD), jnp.float32)
    for side in range(SIDES):
        sums = []
        for member in range(2):
            stat = got_ref[member * SIDES + side, :, GROUP * HD :].astype(jnp.float32)
            sums.append(stat + pltpu.roll(stat, HD - 32, 1) + pltpu.roll(stat, HD - 64, 1))
        high = jnp.maximum(sums[0], sums[1])
        joint = high + jnp.log(jnp.exp(sums[0] - high) + jnp.exp(sums[1] - high))
        logs = jnp.where(lane // GROUP == side, joint, logs)
        share = [jnp.exp(part - joint) for part in sums]
        for head in range(GROUP):
            cols = slice(head * HD, (head + 1) * HD)
            mixed_ref[:, side * GROUP * HD + head * HD : side * GROUP * HD + (head + 1) * HD] = (
                got_ref[side, :, cols].astype(jnp.float32) * share[0][:, head : head + 1]
                + got_ref[SIDES + side, :, cols].astype(jnp.float32)
                * share[1][:, head : head + 1]
            ).astype(jnp.bfloat16)
    log_ref[...] = logs[:, :HQ]


def merge(got):
    whole = pl.BlockSpec(memory_space=pltpu.VMEM)
    return pl.pallas_call(
        merge_body,
        out_shape=(
            jax.ShapeDtypeStruct((64, HQ * HD), jnp.bfloat16),
            jax.ShapeDtypeStruct((64, HQ), jnp.float32),
        ),
        in_specs=[whole],
        out_specs=(whole, whole),
        name="merge",
    )(got)


def per_device(queries, key_states, value_states):
    span = lax.axis_index("qrow")
    column = lax.axis_index("kcol")
    slot = column % 4
    core = column % 2
    half = span // 4
    low = jnp.minimum(span, SPANS - 1 - span)
    info = jnp.stack([low, SPANS - 1 - low, core, half, slot]).astype(jnp.int32)

    pieces = jnp.concatenate(
        [key_states.reshape(64, KVH, HD), value_states.reshape(64, KVH, HD)], axis=2
    ).transpose(1, 0, 2)
    pieces = jnp.broadcast_to(pieces[:, None], (KVH, 8, 64, 2 * HD)).reshape(32, 64, 2 * HD)
    own = lax.all_to_all(pieces, EVERY, 0, 0, axis_index_groups=KEY_GROUPS)
    own = own.reshape(8, 256, 2 * HD)

    sent = queries.reshape(4, SLOTS, 64, 2 * HD).transpose(1, 0, 2, 3).reshape(4, 256, 2 * HD)
    sent = jnp.concatenate([sent, sent], axis=0)
    q_pieces = lax.all_to_all(sent, EVERY, 0, 0, axis_index_groups=QUERY_GROUPS)

    other = lax.ppermute(own, EVERY, [(i, i ^ 1) for i in range(128)])
    partial = attend(info, q_pieces, own, other)
    got = lax.all_to_all(partial, EVERY, 0, 0, axis_index_groups=OUTPUT_GROUPS)
    return merge(got)


def solution(mesh):
    placed = (P("qrow", "kcol"), P(("kcol", "qrow"), None), P(("kcol", "qrow"), None))
    return jax.shard_map(
        per_device,
        mesh=mesh,
        in_specs=placed,
        out_specs=(P(("qrow", "kcol"), None), P(("qrow", "kcol"), None)),
        check_vma=False,
    )
```

time: 530 us -> 106 us (0.20)
  the two profiles are of different devices: /device:TPU:2 before, /device:TPU:0 now
where the time goes in v1:
time: 106 us
  waiting for transfers between devices  38.5 us (36%)
  Pallas kernels  26.3 us (25%)
  blocking collectives  21.5 us (20%)
  starting transfers between devices  12.9 us (12%)
  local copies, waits for them, and re-layouts  4.4 us (4%)
  other arithmetic  1.13 us (1%)
    pallas_call x1, Pallas kernels, attend(): pl.pallas_call(attend_body, out_shape=jax.ShapeDtypeStruct((8, 64, WIDE),...  22.9 us
    all_to_all x1, blocking collectives, per_device(): got = lax.all_to_all(partial, EVERY, 0, 0, axis_index_groups=OUTPUT_GROUPS)  21.5 us
    all_to_all x1, waiting for transfers between devices, per_device(): q_pieces = lax.all_to_all(sent, EVERY, 0, 0, axis_index_groups=QUERY_GROUPS)  20.5 us
    all_to_all x1, waiting for transfers between devices, per_device(): own = lax.all_to_all(pieces, EVERY, 0, 0, axis_index_groups=KEY_GROUPS)  18.1 us
    all_to_all x1, starting transfers between devices, per_device(): own = lax.all_to_all(pieces, EVERY, 0, 0, axis_index_groups=KEY_GROUPS)  9.39 us
    all_to_all x1, starting transfers between devices, per_device(): q_pieces = lax.all_to_all(sent, EVERY, 0, 0, axis_index_groups=QUERY_GROUPS)  3.56 us
    pallas_call x1, Pallas kernels, merge(): pl.pallas_call(merge_body, out_shape=(jax.ShapeDtypeStruct((64, HQ * HD),...  3.47 us
  transfers between devices with their start and end apart: 3, of which 2 were waited for; matrix products, arithmetic and copies ran while one was open for 1% of the time, Pallas kernels for 0%

profile of v1, /device:TPU:0, one launch (start us, length us, event | category | flops | bytes accessed | tf_op | source)
XLA Modules:
  0.0 105.6 jit_solution(18163805980336237899)
XLA Ops:
  0.6 0.9 reshape.25
  1.5 0.9 reshape.26
  2.4 0.1 maximum_bitcast_fusion
  2.5 1.1 %broadcast_in_dim.2 = bf16[4,8,64,256]{3,2,1,0:T(8,128)(2,1)} broadcast(bf16[4,64,256]{2,1,0:T(8,128)(2,1)S(1)} %copy.6), dimensions={0,2,3} | broadcast | bytes 1179648 | tf_op jit(solution)/shard_map/broadcast_in_dim | solution.py:209
  3.5 0.0 copy-start
  3.5 9.4 %all-to-all-start.1 = ((bf16[32,64,256]{2,1,0:T(8,128)(2,1)}), bf16[32,64,256]{2,1,0:T(8,128)(2,1)S(1)}, u32[]{:S(2)}, u32[]{:S(2)}) async-start(bf16[32,64,256]{2,1,0:T(8,128)(2,1)} %bitcast.9), calls=%async_computation.1 | async-start | bytes 2097152 | tf_op jit(solution)/shard_map/all_to_all | solution.py:210
  12.9 0.0 copy-done
  13.0 18.1 %all-to-all-done.1 = bf16[32,64,256]{2,1,0:T(8,128)(2,1)S(1)} async-done(((bf16[32,64,256]{2,1,0:T(8,128)(2,1)}), bf16[32,64,256]{2,1,0:T(8,128)(2,1)S(1)}, u32[]{:S(2)}, u32[]{:S(2)}) %all-to-all-start.1) | async-done | bytes 1048608 | tf_op jit(solution)/shard_map/all_to_all | solution.py:210
  31.1 0.0 collective-permute-start
  31.1 1.1 %pad_maximum_fusion = bf16[8,256,256]{2,1,0:T(8,128)(2,1)} fusion(bf16[4,256,256]{2,1,0:T(8,128)(2,1)S(1)} %bitcast.15), kind=kLoop, calls=%fused_computation | loop fusion | flops 524288 | bytes 1572864 | tf_op jit(solution)/shard_map/concatenate | solution.py:214
  32.1 3.6 %all-to-all-start = ((bf16[8,256,256]{2,1,0:T(8,128)(2,1)}), bf16[8,256,256]{2,1,0:T(8,128)(2,1)S(1)}, u32[]{:S(2)}, u32[]{:S(2)}) async-start(bf16[8,256,256]{2,1,0:T(8,128)(2,1)} %pad_maximum_fusion), calls=%async_computation | async-start | bytes 2097152 | tf_op jit(solution)/shard_map/all_to_all | solution.py:215
  35.7 0.1 stack.23.info
  35.8 20.5 %all-to-all-done.q_ref = bf16[8,256,256]{2,1,0:T(8,128)(2,1)S(1)} async-done(((bf16[8,256,256]{2,1,0:T(8,128)(2,1)}), bf16[8,256,256]{2,1,0:T(8,128)(2,1)S(1)}, u32[]{:S(2)}, u32[]{:S(2)}) %all-to-all-start) | async-done | bytes 1048608 | tf_op jit(solution)/shard_map/all_to_all | solution.py:215
  56.3 0.0 collective-permute-done.second_ref
  56.3 22.9 %attend.1 = bf16[8,64,1152]{2,1,0:T(8,128)(2,1)S(1)} custom-call(s32[5]{0:T(128)S(1)} %stack.23.info, bf16[8,256,256]{2,1,0:T(8,128)(2,1)S(1)} %all-to-all-done.q_ref, bf16[8,256,256]{2,1,0:T(8,128)(2,1)S(1)} %bitcast.14, bf16[8,256,256]{2,1,0:T(8,128)(2,1)S(1)} %collective-permute-done.second_ref), custom_call_target="tpu_custom_call" | custom-call | flops 4831838208 | bytes 4194304 | tf_op jit(solution)/shard_map/attend/pallas_call | solution.py:139
  79.2 21.5 %all_to_all.15.got_ref = bf16[8,64,1152]{2,1,0:T(8,128)(2,1)} all-to-all(bf16[8,64,1152]{2,1,0:T(8,128)(2,1)S(1)} %attend.1), channel_id=1, replica_groups={{0,4,8,12,112,116,120,124},{1,5,9,13,113,117,121,125},{2,6,10,14,114,11..., dimensions={0} | all-to-all | bytes 2359296 | tf_op jit(solution)/shard_map/all_to_all | solution.py:219
  100.7 3.5 %merge.1 = (bf16[64,4096]{1,0:T(8,128)(2,1)}, f32[64,32]{1,0:T(8,128)}) custom-call(bf16[8,64,1152]{2,1,0:T(8,128)(2,1)} %all_to_all.15.got_ref), custom_call_target="tpu_custom_call" | custom-call | tf_op jit(solution)/shard_map/merge/pallas_call | solution.py:185
  104.1 1.4 %copy.7 = f32[64,32]{0,1:T(8,128)} copy(f32[64,32]{1,0:T(8,128)} %get-tuple-element.3) | data formatting | bytes 16384 | tf_op jit(solution)/shard_map/merge/pallas_call | solution.py:185
  (2 shorter events, 0.1 us)
Async XLA Ops:
  3.5 9.4 %copy-start = (bf16[1024,256]{1,0:T(8,128)(2,1)S(1)}, bf16[1024,256]{1,0:T(8,128)(2,1)}, u32[]{:S(2)}) copy-start(bf16[1024,256]{1,0:T(8,128)(2,1)} %param.3) | copy-start | bytes 1572868
  3.5 27.5 %all-to-all-start.1 = ((bf16[32,64,256]{2,1,0:T(8,128)(2,1)}), bf16[32,64,256]{2,1,0:T(8,128)(2,1)S(1)}, u32[]{:S(2)}, u32[]{:S(2)}) async-start(bf16[32,64,256]{2,1,0:T(8,128)(2,1)} %bitcast.9), calls=%async_computation.1 | async-start | bytes 2097152 | tf_op jit(solution)/shard_map/all_to_all | solution.py:210
  31.1 25.2 %collective-permute-start = (bf16[8,256,256]{2,1,0:T(8,128)(2,1)S(1)}, bf16[8,256,256]{2,1,0:T(8,128)(2,1)S(1)}, u32[]{:S(2)}, u32[]{:S(2)}) collective-permute-start(bf16[8,256,256]{2,1,0:T(8,128)(2,1)S(1)} %bitcast.13), channel_id=1, source_target_pairs={{0,1},{1,0},{2,3},{3,2},{4,5},{5,4},{6,7},{7,6},{8,9},{9,8},{10,11... | collective-permute-start | bytes 3145736 | tf_op jit(solution)/shard_map/ppermute | solution.py:217
  32.1 24.2 %all-to-all-start = ((bf16[8,256,256]{2,1,0:T(8,128)(2,1)}), bf16[8,256,256]{2,1,0:T(8,128)(2,1)S(1)}, u32[]{:S(2)}, u32[]{:S(2)}) async-start(bf16[8,256,256]{2,1,0:T(8,128)(2,1)} %pad_maximum_fusion), calls=%async_computation | async-start | bytes 2097152 | tf_op jit(solution)/shard_map/all_to_all | solution.py:215

commit v2 on v1

v2 whole, which is shorter than its diff:
```python
import functools
import math

import jax
import jax.numpy as jnp
from jax import lax
from jax.experimental import pallas as pl
from jax.experimental.pallas import tpu as pltpu
from jax.sharding import PartitionSpec as P

HQ = 32
KVH = 4
HD = 128
GROUP = 8
EVERY = ("qrow", "kcol")
SPANS = 8
DEVICES = 128
SIDES = 4

NEG_FILL = -1e30
LOG2E = math.log2(math.e)
LN2 = math.log(2.0)
HELD = 4
WIDE = HELD * HD + HD


def device_at(span, side, slot):
    return span * 16 + side * 4 + slot


KEY_GROUPS = [
    [
        device_at(half * 4 + near, side, xh * 2 + core)
        for side in range(SIDES)
        for xh in range(2)
        for near in range(4)
    ]
    for half in range(2)
    for core in range(2)
]
OUTPUT_GROUPS = [
    [
        device_at(span, side, xh * 2 + core)
        for span in (low, low ^ 6)
        for side in range(SIDES)
        for xh in range(2)
    ]
    for low in range(SPANS // 2)
    for core in range(2)
]


def pack_body(key_ref, value_ref, out_ref):
    for side in range(SIDES):
        cols = slice(side * HD, (side + 1) * HD)
        for copy in range(8):
            out_ref[side * 8 + copy, :, :HD] = key_ref[:, cols]
            out_ref[side * 8 + copy, :, HD:] = value_ref[:, cols]


def pack(key_states, value_states):
    whole = pl.BlockSpec(memory_space=pltpu.VMEM)
    return pl.pallas_call(
        pack_body,
        out_shape=jax.ShapeDtypeStruct((32, 64, 2 * HD), jnp.bfloat16),
        in_specs=[whole, whole],
        out_specs=whole,
        name="pack",
    )(key_states, value_states)


def split_body(place, q_ref, *out_refs):
    core = place[1] & 1
    for shift in range(2):
        for piece in range(8):
            at = pl.multiple_of(piece * 128 + (core ^ shift) * 64, 64)
            out_refs[shift][piece] = q_ref[pl.ds(at, 64), :]


def split(place, queries):
    whole = pl.BlockSpec(memory_space=pltpu.VMEM)
    return pl.pallas_call(
        split_body,
        out_shape=[jax.ShapeDtypeStruct((8, 64, 2 * HD), jnp.bfloat16)] * 2,
        in_specs=[pl.BlockSpec(memory_space=pltpu.SMEM), whole],
        out_specs=[whole] * 2,
        cost_estimate=pl.CostEstimate(
            flops=2 * 10**10, bytes_accessed=2**20, transcendentals=0
        ),
        name="split",
    )(place, queries)


def columns(wide):
    return [wide[:, i * HD : (i + 1) * HD] for i in range(wide.shape[1] // HD)]


def row_peak(parts):
    return jnp.max(functools.reduce(jnp.maximum, parts), axis=1, keepdims=True)


def rounded(parts):
    return jnp.concatenate([part.astype(jnp.bfloat16) for part in parts], axis=1)


def attend_body(place, *refs):
    q_refs = refs[:4]
    own_ref, other_ref, o_ref, q_all, keys, values, acc, top = refs[4:]
    row, column = place[0], place[1]
    half, core = row >> 2, column & 1

    for ref, part in ((own_ref, core), (other_ref, 1 - core)):
        held = pl.ds(pl.multiple_of(part * 256, 256), 256)
        for block in range(8):
            keys[block, held, :] = ref[block, :, :HD]
            values[block, held, :HD] = ref[block, :, HD:]
    for block in range(8):
        values[block, :, HD:] = jnp.ones((512, HD), jnp.bfloat16)

    def score(rows, block, width):
        return lax.dot_general(
            q_all[rows, :],
            keys[block, :width, :],
            (((1,), (1,)), ((), ())),
            preferred_element_type=jnp.float32,
        ) * (LOG2E / math.sqrt(HD))

    def weigh(rows, scores):
        parts = columns(scores)
        old = top[rows, :]
        new = jnp.maximum(old, row_peak(parts))
        top[rows, :] = new
        return rounded([jnp.exp2(part - new) for part in parts]), jnp.exp2(old - new)

    def add(rows, block, weights, scale):
        fresh = jnp.dot(weights, values[block], preferred_element_type=jnp.float32)
        acc[rows, :HD] = acc[rows, :HD] * scale + fresh[:, :HD]
        acc[rows, HD:] = acc[rows, HD:] * scale + fresh[:, HD:]

    tiles = [slice(tile * 512, (tile + 1) * 512) for tile in range(4)]
    lane = lax.broadcasted_iota(jnp.int32, (64, HD), 1)
    in_tile = lax.broadcasted_iota(jnp.int32, (512, HD), 0)
    in_row = (in_tile >> 8) * 128 + (in_tile & 63)
    in_col = lax.broadcasted_iota(jnp.int32, (512, HD), 1)
    for turn in range(2):
        span = row if turn == 0 else row ^ 6
        member = (row >> 2) ^ turn
        for shift in range(2):
            for piece in range(8):
                for head in range(2):
                    at = piece * 256 + (core ^ shift) * 128 + head * 64
                    q_all[pl.ds(pl.multiple_of(at, 64), 64), :] = q_refs[turn * 2 + shift][
                        piece, :, head * HD : (head + 1) * HD
                    ]

        for tile, rows in enumerate(tiles):
            width = 256 if tile < 2 else 512
            parts = columns(score(rows, span, width))
            reach = in_row + (tile % 2) * 256 + core * 64 - half * 256
            keep = [in_col + i * HD <= reach for i in range(2)]
            parts[-2:] = [jnp.where(k, p, NEG_FILL) for k, p in zip(keep, parts[-2:])]
            peak = jnp.broadcast_to(row_peak(parts), (512, HD))
            weights = [jnp.exp2(part - peak) for part in parts]
            weights[-2:] = [jnp.where(k, w, 0.0) for k, w in zip(keep, weights[-2:])]
            top[rows, :] = peak
            acc[rows, :] = jnp.dot(
                rounded(weights), values[span, :width, :], preferred_element_type=jnp.float32
            )

        @pl.loop(0, span)
        def _(block):
            ready = score(tiles[0], block, 512)
            waiting = None
            for tile, rows in enumerate(tiles):
                later = score(tiles[tile + 1], block, 512) if tile < 3 else None
                now = weigh(rows, ready)
                if waiting is not None:
                    add(tiles[tile - 1], block, *waiting)
                waiting, ready = now, later
            add(tiles[3], block, *waiting)

        for piece in range(8):
            peaks = jnp.zeros((64, HD), jnp.float32)
            totals = jnp.zeros((64, HD), jnp.float32)
            for head in range(HELD):
                at = piece * 256 + head * 64
                rows = slice(at, at + 64)
                total = acc[rows, HD:]
                o_ref[member * 8 + piece, :, head * HD : (head + 1) * HD] = (
                    acc[rows, :HD] / jnp.where(total > 0, total, 1.0)
                ).astype(jnp.bfloat16)
                mine = lane % HELD == head
                peaks = jnp.where(mine, top[rows, :], peaks)
                totals = jnp.where(mine, total, totals)
            some = totals > 0
            stat = jnp.where(
                some, (peaks + jnp.log2(jnp.where(some, totals, 1.0))) * LN2, NEG_FILL
            )
            coarse = stat.astype(jnp.bfloat16).astype(jnp.float32)
            middle = (stat - coarse).astype(jnp.bfloat16).astype(jnp.float32)
            fine = stat - coarse - middle
            o_ref[member * 8 + piece, :, HELD * HD :] = jnp.where(
                lane < 32, coarse, jnp.where(lane < 64, middle, fine)
            ).astype(jnp.bfloat16)


def attend(place, q_pieces, own, other):
    whole = pl.BlockSpec(memory_space=pltpu.VMEM)
    return pl.pallas_call(
        attend_body,
        out_shape=jax.ShapeDtypeStruct((16, 64, WIDE), jnp.bfloat16),
        in_specs=[pl.BlockSpec(memory_space=pltpu.SMEM)] + [whole] * 6,
        out_specs=whole,
        scratch_shapes=[
            pltpu.VMEM((2048, HD), jnp.bfloat16),
            pltpu.VMEM((8, 512, HD), jnp.bfloat16),
            pltpu.VMEM((8, 512, 2 * HD), jnp.bfloat16),
            pltpu.VMEM((2048, 2 * HD), jnp.float32),
            pltpu.VMEM((2048, HD), jnp.float32),
        ],
        compiler_params=pltpu.CompilerParams(vmem_limit_bytes=48 * 2**20),
        cost_estimate=pl.CostEstimate(
            flops=36 * 4 * 512 * 512 * HD,
            bytes_accessed=4 * 2**20,
            transcendentals=36 * 512 * 512,
        ),
        name="attend",
    )(place, *q_pieces, own, other)


def merge_body(got_ref, mixed_ref, log_ref):
    side = pl.program_id(0)
    lane = lax.broadcasted_iota(jnp.int32, (64, HD), 1)
    joints = []
    for xh in range(2):
        sums = []
        for member in range(2):
            stat = got_ref[member, xh, :, HELD * HD :].astype(jnp.float32)
            sums.append(stat + pltpu.roll(stat, HD - 32, 1) + pltpu.roll(stat, HD - 64, 1))
        high = jnp.maximum(sums[0], sums[1])
        joint = high + jnp.log(jnp.exp(sums[0] - high) + jnp.exp(sums[1] - high))
        joints.append(joint)
        share = [jnp.exp(part - joint) for part in sums]
        for head in range(HELD):
            cols = slice(head * HD, (head + 1) * HD)
            into = slice((xh * HELD + head) * HD, (xh * HELD + head + 1) * HD)
            mixed_ref[:, into] = (
                got_ref[0, xh, :, cols].astype(jnp.float32) * share[0][:, head : head + 1]
                + got_ref[1, xh, :, cols].astype(jnp.float32) * share[1][:, head : head + 1]
            ).astype(jnp.bfloat16)
    logs = jnp.where(lane < HELD, joints[0], joints[1])
    log_ref[pl.ds(pl.multiple_of(side * GROUP, GROUP), GROUP), :] = logs.T[:GROUP, :]


def merge(got):
    return pl.pallas_call(
        merge_body,
        grid=(SIDES,),
        out_shape=(
            jax.ShapeDtypeStruct((64, HQ * HD), jnp.bfloat16),
            jax.ShapeDtypeStruct((HQ, 64), jnp.float32),
        ),
        in_specs=[pl.BlockSpec((2, 2, 64, WIDE), lambda side: (0, side, 0, 0))],
        out_specs=(
            pl.BlockSpec((64, GROUP * HD), lambda side: (0, side)),
            pl.BlockSpec((HQ, 64), lambda side: (0, 0)),
        ),
        name="merge",
    )(got.reshape(2, 2 * SIDES, 64, WIDE))


def per_device(queries, key_states, value_states):
    row = lax.axis_index("qrow")
    column = lax.axis_index("kcol")
    place = jnp.stack([row, column])

    own = lax.all_to_all(
        pack(key_states, value_states), EVERY, 0, 0, axis_index_groups=KEY_GROUPS
    ).reshape(8, 256, 2 * HD)

    by_shift = split(place, queries)
    q_pieces = []
    for turn in range(2):
        for shift in range(2):
            piece = by_shift[shift]
            if turn or shift:
                pairs = [(i, i ^ shift ^ (96 * turn)) for i in range(DEVICES)]
                piece = lax.ppermute(piece, EVERY, pairs)
            q_pieces.append(piece)

    own, q_pieces = lax.optimization_barrier((own, q_pieces))
    other = lax.ppermute(own, EVERY, [(i, i ^ 1) for i in range(DEVICES)])
    partial = attend(place, q_pieces, own, other)
    got = lax.all_to_all(partial, EVERY, 0, 0, axis_index_groups=OUTPUT_GROUPS)
    mixed, logs = merge(got)
    return (mixed, logs.T)


def solution(mesh):
    placed = (P("qrow", "kcol"), P(("kcol", "qrow"), None), P(("kcol", "qrow"), None))
    return jax.shard_map(
        per_device,
        mesh=mesh,
        in_specs=placed,
        out_specs=(P(("qrow", "kcol"), None), P(("qrow", "kcol"), None)),
        check_vma=False,
    )
```

time: 106 us -> 84.1 us (0.79)
  the two profiles are of different devices: /device:TPU:0 before, /device:TPU:2 now
where the time goes in v2:
time: 84.1 us; the launch traced here: 83.7 us
  blocking collectives  29.8 us (35%)
  Pallas kernels  25.5 us (30%)
  starting transfers between devices  13.3 us (16%)
  waiting for transfers between devices  12.8 us (15%)
  local copies, waits for them, and re-layouts  0.95 us (1%)
    all_to_all x1, blocking collectives, per_device(): got = lax.all_to_all(partial, EVERY, 0, 0, axis_index_groups=OUTPUT_GROUPS)  29.8 us
    pallas_call x1, Pallas kernels, attend(): pl.pallas_call(attend_body, out_shape=jax.ShapeDtypeStruct((16, 64, WIDE)...  17.5 us
    ppermute x3, waiting for transfers between devices, per_device(): piece = lax.ppermute(piece, EVERY, pairs)  10.5 us
    all_to_all x1, starting transfers between devices, per_device(): lax.all_to_all(pack(key_states, value_states), EVERY, 0, 0, axis_index_gr...  9.47 us
    pallas_call x1, Pallas kernels, merge(): pl.pallas_call(merge_body, grid=(SIDES,), out_shape=(jax.ShapeDtypeStruct...  4.17 us
    ppermute x3, starting transfers between devices, per_device(): piece = lax.ppermute(piece, EVERY, pairs)  3.35 us
    ppermute x1, waiting for transfers between devices, per_device(): other = lax.ppermute(own, EVERY, [(i, i ^ 1) for i in range(DEVICES)])  2.29 us
    pallas_call x1, Pallas kernels, pack(): pl.pallas_call(pack_body, out_shape=jax.ShapeDtypeStruct((32, 64, 2 * HD)...  1.97 us
  transfers between devices with their start and end apart: 5, of which 3 were waited for; matrix products, arithmetic and copies ran while one was open for 1% of the time, Pallas kernels for 2%

profile of v2, /device:TPU:2, one launch (start us, length us, event | category | flops | bytes accessed | tf_op | source)
XLA Modules:
  0.0 83.7 jit_solution(148949971355186022)
XLA Ops:
  0.6 2.0 %pack.1 = bf16[32,64,256]{2,1,0:T(8,128)(2,1)} custom-call(bf16[64,512]{1,0:T(8,128)(2,1)} %key_ref.1, bf16[64,512]{1,0:T(8,128)(2,1)} %value_ref.1), custom_call_target="tpu_custom_call" | custom-call | tf_op jit(solution)/shard_map/pack/pallas_call | solution.py:63
  2.6 9.5 %all-to-all-start = ((bf16[32,64,256]{2,1,0:T(8,128)(2,1)}), bf16[32,64,256]{2,1,0:T(8,128)(2,1)S(1)}, u32[]{:S(2)}, u32[]{:S(2)}) async-start(bf16[32,64,256]{2,1,0:T(8,128)(2,1)} %pack.1), calls=%async_computation | async-start | bytes 2097152 | tf_op jit(solution)/shard_map/all_to_all | solution.py:277
  12.1 0.6 pad_add_fusion.place
  12.7 0.0 copy-start.1
  12.7 1.9 %split.1 = (bf16[8,64,256]{2,1,0:T(8,128)(2,1)}, bf16[8,64,256]{2,1,0:T(8,128)(2,1)}) custom-call(s32[2]{0:T(128)} %pad_add_fusion.place, bf16[1024,256]{1,0:T(8,128)(2,1)} %q_ref.1), custom_call_target="tpu_custom_call" | custom-call | flops 20000000000 | bytes 1048576 | tf_op jit(solution)/shard_map/split/pallas_call | solution.py:82
  14.6 2.9 %collective-permute-start.1 = (bf16[8,64,256]{2,1,0:T(8,128)(2,1)}, bf16[8,64,256]{2,1,0:T(8,128)(2,1)S(1)}, u32[]{:S(2)}, u32[]{:S(2)}) collective-permute-start(bf16[8,64,256]{2,1,0:T(8,128)(2,1)} %get-tuple-element.13.refs_0_), channel_id=1, source_target_pairs={{0,96},{1,97},{2,98},{3,99},{4,100},{5,101},{6,102},{7,103},{8,104... | collective-permute-start | bytes 786440 | tf_op jit(solution)/shard_map/ppermute | solution.py:288
  17.5 0.0 collective-permute-start.2
  17.5 0.4 collective-permute-start
  17.9 7.1 %collective-permute-done.1.refs_2_ = bf16[8,64,256]{2,1,0:T(8,128)(2,1)S(1)} collective-permute-done((bf16[8,64,256]{2,1,0:T(8,128)(2,1)}, bf16[8,64,256]{2,1,0:T(8,128)(2,1)S(1)}, u32[]{:S(2)}, u32[]{:S(2)}) %collective-permute-start.1) | collective-permute-done | bytes 262176 | tf_op jit(solution)/shard_map/ppermute | solution.py:288
  25.0 3.4 %collective-permute-done.2.refs_3_ = bf16[8,64,256]{2,1,0:T(8,128)(2,1)S(1)} collective-permute-done((bf16[8,64,256]{2,1,0:T(8,128)(2,1)}, bf16[8,64,256]{2,1,0:T(8,128)(2,1)S(1)}, u32[]{:S(2)}, u32[]{:S(2)}) %collective-permute-start.2) | collective-permute-done | bytes 262176 | tf_op jit(solution)/shard_map/ppermute | solution.py:288
  28.4 0.0 collective-permute-done.refs_1_
  28.4 0.0 all-to-all-done
  28.4 0.5 collective-permute-start.3
  28.9 2.3 %collective-permute-done.3.refs_5_ = bf16[8,256,256]{2,1,0:T(8,128)(2,1)S(1)} collective-permute-done((bf16[8,256,256]{2,1,0:T(8,128)(2,1)S(1)}, bf16[8,256,256]{2,1,0:T(8,128)(2,1)S(1)}, u32[]{:S(2)}, u32[]{:S(2)}) %collective-permute-start.3) | collective-permute-done | bytes 1048608 | tf_op jit(solution)/shard_map/ppermute | solution.py:292
  31.2 0.0 copy-done.1
  31.2 0.0 copy-start
  31.2 0.9 %copy-done = bf16[8,64,256]{2,1,0:T(8,128)(2,1)S(1)} copy-done((bf16[8,64,256]{2,1,0:T(8,128)(2,1)S(1)}, bf16[8,64,256]{2,1,0:T(8,128)(2,1)}, u32[]{:S(2)}) %copy-start) | copy-done | bytes 262168
  32.2 17.5 %attend.1 = bf16[16,64,640]{2,1,0:T(8,128)(2,1)S(1)} custom-call(s32[2]{0:T(128)S(1)} %copy-done.1, bf16[8,64,256]{2,1,0:T(8,128)(2,1)S(1)} %copy-done, bf16[8,64,256]{2,1,0:T(8,128)(2,1)S(1)} %collective-permute-done.refs_1_, bf16[8,64,256]{2,1,0:T(8,128)(2,1)S(1)} %collective-permute-done.1.refs_2_, ...), custom_call_target="tpu_custom_call" | custom-call | flops 4831838208 | bytes 4194304 | tf_op jit(solution)/shard_map/attend/pallas_call | solution.py:209
  49.7 29.8 %all_to_all.10 = bf16[16,64,640]{2,1,0:T(8,128)(2,1)} all-to-all(bf16[16,64,640]{2,1,0:T(8,128)(2,1)S(1)} %attend.1), channel_id=1, replica_groups={{0,2,4,6,8,10,12,14,96,98,100,102,104,106,108,110},{1,3,5,7,9,11,13,15,..., dimensions={0} | all-to-all | bytes 2621440 | tf_op jit(solution)/shard_map/all_to_all | solution.py:294
  79.5 4.2 %merge.1 = (bf16[64,4096]{1,0:T(8,128)(2,1)}, f32[32,64]{1,0:T(8,128)}) custom-call(bf16[2,8,64,640]{3,2,1,0:T(8,128)(2,1)} %bitcast.7), custom_call_target="tpu_custom_call" | custom-call | tf_op jit(solution)/shard_map/merge/pallas_call | solution.py:256
Async XLA Ops:
  2.6 25.8 %all-to-all-start = ((bf16[32,64,256]{2,1,0:T(8,128)(2,1)}), bf16[32,64,256]{2,1,0:T(8,128)(2,1)S(1)}, u32[]{:S(2)}, u32[]{:S(2)}) async-start(bf16[32,64,256]{2,1,0:T(8,128)(2,1)} %pack.1), calls=%async_computation | async-start | bytes 2097152 | tf_op jit(solution)/shard_map/all_to_all | solution.py:277
  12.7 18.5 %copy-start.1 = (s32[2]{0:T(128)S(1)}, s32[2]{0:T(128)}, u32[]{:S(2)}) copy-start(s32[2]{0:T(128)} %pad_add_fusion.place) | copy-start | bytes 28
  14.6 10.4 %collective-permute-start.1 = (bf16[8,64,256]{2,1,0:T(8,128)(2,1)}, bf16[8,64,256]{2,1,0:T(8,128)(2,1)S(1)}, u32[]{:S(2)}, u32[]{:S(2)}) collective-permute-start(bf16[8,64,256]{2,1,0:T(8,128)(2,1)} %get-tuple-element.13.refs_0_), channel_id=1, source_target_pairs={{0,96},{1,97},{2,98},{3,99},{4,100},{5,101},{6,102},{7,103},{8,104... | collective-permute-start | bytes 786440 | tf_op jit(solution)/shard_map/ppermute | solution.py:288
  17.5 10.9 %collective-permute-start.2 = (bf16[8,64,256]{2,1,0:T(8,128)(2,1)}, bf16[8,64,256]{2,1,0:T(8,128)(2,1)S(1)}, u32[]{:S(2)}, u32[]{:S(2)}) collective-permute-start(bf16[8,64,256]{2,1,0:T(8,128)(2,1)} %get-tuple-element.12), channel_id=1, source_target_pairs={{0,97},{1,96},{2,99},{3,98},{4,101},{5,100},{6,103},{7,102},{8,105... | collective-permute-start | bytes 786440 | tf_op jit(solution)/shard_map/ppermute | solution.py:288
  17.5 10.9 %collective-permute-start = (bf16[8,64,256]{2,1,0:T(8,128)(2,1)}, bf16[8,64,256]{2,1,0:T(8,128)(2,1)S(1)}, u32[]{:S(2)}, u32[]{:S(2)}) collective-permute-start(bf16[8,64,256]{2,1,0:T(8,128)(2,1)} %get-tuple-element.12), channel_id=1, source_target_pairs={{0,1},{1,0},{2,3},{3,2},{4,5},{5,4},{6,7},{7,6},{8,9},{9,8},{10,11... | collective-permute-start | bytes 786440 | tf_op jit(solution)/shard_map/ppermute | solution.py:288
  28.4 2.8 %collective-permute-start.3 = (bf16[8,256,256]{2,1,0:T(8,128)(2,1)S(1)}, bf16[8,256,256]{2,1,0:T(8,128)(2,1)S(1)}, u32[]{:S(2)}, u32[]{:S(2)}) collective-permute-start(bf16[8,256,256]{2,1,0:T(8,128)(2,1)S(1)} %bitcast.5), channel_id=1, source_target_pairs={{0,1},{1,0},{2,3},{3,2},{4,5},{5,4},{6,7},{7,6},{8,9},{9,8},{10,11... | collective-permute-start | bytes 3145736 | tf_op jit(solution)/shard_map/ppermute | solution.py:292
  31.2 1.0 %copy-start = (bf16[8,64,256]{2,1,0:T(8,128)(2,1)S(1)}, bf16[8,64,256]{2,1,0:T(8,128)(2,1)}, u32[]{:S(2)}) copy-start(bf16[8,64,256]{2,1,0:T(8,128)(2,1)} %get-tuple-element.13.refs_0_) | copy-start | bytes 786436

commit v3 on v2

--- a/solution.py
+++ b/solution.py
@@ -21,7 +21,7 @@
 LOG2E = math.log2(math.e)
 LN2 = math.log(2.0)
 HELD = 4
-WIDE = HELD * HD + HD
+ROWS = 72
 
 
 def device_at(span, side, slot):
@@ -31,9 +31,9 @@
 KEY_GROUPS = [
     [
         device_at(half * 4 + near, side, xh * 2 + core)
+        for near in range(4)
+        for xh in range(2)
         for side in range(SIDES)
-        for xh in range(2)
-        for near in range(4)
     ]
     for half in range(2)
     for core in range(2)
@@ -54,8 +54,8 @@
     for side in range(SIDES):
         cols = slice(side * HD, (side + 1) * HD)
         for copy in range(8):
-            out_ref[side * 8 + copy, :, :HD] = key_ref[:, cols]
-            out_ref[side * 8 + copy, :, HD:] = value_ref[:, cols]
+            out_ref[copy * SIDES + side, :, :HD] = key_ref[:, cols]
+            out_ref[copy * SIDES + side, :, HD:] = value_ref[:, cols]
 
 
 def pack(key_states, value_states):
@@ -87,6 +87,7 @@
         cost_estimate=pl.CostEstimate(
             flops=2 * 10**10, bytes_accessed=2**20, transcendentals=0
         ),
+        compiler_params=pltpu.CompilerParams(vmem_limit_bytes=8 * 2**20),
         name="split",
     )(place, queries)
 
@@ -110,10 +111,13 @@
     half, core = row >> 2, column & 1
 
     for ref, part in ((own_ref, core), (other_ref, 1 - core)):
-        held = pl.ds(pl.multiple_of(part * 256, 256), 256)
         for block in range(8):
-            keys[block, held, :] = ref[block, :, :HD]
-            values[block, held, :HD] = ref[block, :, HD:]
+            side, xh = block // 2, block % 2
+            for near in range(4):
+                held = pl.ds(pl.multiple_of(part * 256 + near * 64, 64), 64)
+                piece = (near * 2 + xh) * SIDES + side
+                keys[block, held, :] = ref[piece, :, :HD]
+                values[block, held, :HD] = ref[piece, :, HD:]
     for block in range(8):
         values[block, :, HD:] = jnp.ones((512, HD), jnp.bfloat16)
 
@@ -126,14 +130,18 @@
         ) * (LOG2E / math.sqrt(HD))
 
     def weigh(rows, scores):
-        parts = columns(scores)
+        parts = [columns(wide) for wide in scores]
         old = top[rows, :]
-        new = jnp.maximum(old, row_peak(parts))
+        new = jnp.maximum(old, row_peak(sum(parts, [])))
         top[rows, :] = new
-        return rounded([jnp.exp2(part - new) for part in parts]), jnp.exp2(old - new)
-
-    def add(rows, block, weights, scale):
-        fresh = jnp.dot(weights, values[block], preferred_element_type=jnp.float32)
+        weights = [rounded([jnp.exp2(part - new) for part in some]) for some in parts]
+        return weights, jnp.exp2(old - new)
+
+    def add(rows, blocks, weights, scale):
+        fresh = sum(
+            jnp.dot(weight, values[block], preferred_element_type=jnp.float32)
+            for weight, block in zip(weights, blocks)
+        )
         acc[rows, :HD] = acc[rows, :HD] * scale + fresh[:, :HD]
         acc[rows, HD:] = acc[rows, HD:] * scale + fresh[:, HD:]
 
@@ -167,48 +175,64 @@
                 rounded(weights), values[span, :width, :], preferred_element_type=jnp.float32
             )
 
-        @pl.loop(0, span)
-        def _(block):
-            ready = score(tiles[0], block, 512)
-            waiting = None
+        def sweep(blocks):
+            def ahead(tile):
+                return [score(tiles[tile], block, 512) for block in blocks]
+
+            ready, waiting = ahead(0), None
             for tile, rows in enumerate(tiles):
-                later = score(tiles[tile + 1], block, 512) if tile < 3 else None
+                later = ahead(tile + 1) if tile < 3 else None
                 now = weigh(rows, ready)
                 if waiting is not None:
-                    add(tiles[tile - 1], block, *waiting)
+                    add(tiles[tile - 1], blocks, *waiting)
                 waiting, ready = now, later
-            add(tiles[3], block, *waiting)
-
-        for piece in range(8):
-            peaks = jnp.zeros((64, HD), jnp.float32)
-            totals = jnp.zeros((64, HD), jnp.float32)
-            for head in range(HELD):
-                at = piece * 256 + head * 64
-                rows = slice(at, at + 64)
-                total = acc[rows, HD:]
-                o_ref[member * 8 + piece, :, head * HD : (head + 1) * HD] = (
-                    acc[rows, :HD] / jnp.where(total > 0, total, 1.0)
-                ).astype(jnp.bfloat16)
-                mine = lane % HELD == head
-                peaks = jnp.where(mine, top[rows, :], peaks)
-                totals = jnp.where(mine, total, totals)
-            some = totals > 0
-            stat = jnp.where(
-                some, (peaks + jnp.log2(jnp.where(some, totals, 1.0))) * LN2, NEG_FILL
-            )
-            coarse = stat.astype(jnp.bfloat16).astype(jnp.float32)
-            middle = (stat - coarse).astype(jnp.bfloat16).astype(jnp.float32)
-            fine = stat - coarse - middle
-            o_ref[member * 8 + piece, :, HELD * HD :] = jnp.where(
-                lane < 32, coarse, jnp.where(lane < 64, middle, fine)
-            ).astype(jnp.bfloat16)
+            add(tiles[3], blocks, *waiting)
+
+        @pl.when((span & 1) == 1)
+        def _():
+            sweep([span - 1])
+
+        @pl.loop(0, span >> 1)
+        def _(pair):
+            sweep([pair * 2, pair * 2 + 1])
+
+        for both in range(4):
+            stats = []
+            for piece in (both * 2, both * 2 + 1):
+                peaks = jnp.zeros((64, HD), jnp.float32)
+                totals = jnp.zeros((64, HD), jnp.float32)
+                for head in range(HELD):
+                    at = piece * 256 + head * 64
+                    rows = slice(at, at + 64)
+                    total = acc[rows, HD:]
+                    o_ref[member * 8 + piece, :64, head * HD : (head + 1) * HD] = (
+                        acc[rows, :HD] / jnp.where(total > 0, total, 1.0)
+                    ).astype(jnp.bfloat16)
+                    mine = lane % HELD == head
+                    peaks = jnp.where(mine, top[rows, :], peaks)
+                    totals = jnp.where(mine, total, totals)
+                some = totals > 0
+                stats.append(
+                    jnp.where(
+                        some, (peaks + jnp.log2(jnp.where(some, totals, 1.0))) * LN2, NEG_FILL
+                    )
+                )
+            by_head = jnp.concatenate(stats, axis=0).T[:8, :]
+            for part in range(2):
+                stat = pltpu.roll(by_head, 64, 1) if part else by_head
+                coarse = stat.astype(jnp.bfloat16).astype(jnp.float32)
+                middle = (stat - coarse).astype(jnp.bfloat16).astype(jnp.float32)
+                fine = stat - coarse - middle
+                o_ref[member * 8 + both * 2 + part, 64:, :] = rounded(
+                    [coarse, middle, fine, jnp.zeros_like(fine)]
+                )
 
 
 def attend(place, q_pieces, own, other):
     whole = pl.BlockSpec(memory_space=pltpu.VMEM)
     return pl.pallas_call(
         attend_body,
-        out_shape=jax.ShapeDtypeStruct((16, 64, WIDE), jnp.bfloat16),
+        out_shape=jax.ShapeDtypeStruct((16, ROWS, HELD * HD), jnp.bfloat16),
         in_specs=[pl.BlockSpec(memory_space=pltpu.SMEM)] + [whole] * 6,
         out_specs=whole,
         scratch_shapes=[
@@ -218,7 +242,7 @@
             pltpu.VMEM((2048, 2 * HD), jnp.float32),
             pltpu.VMEM((2048, HD), jnp.float32),
         ],
-        compiler_params=pltpu.CompilerParams(vmem_limit_bytes=48 * 2**20),
+        compiler_params=pltpu.CompilerParams(vmem_limit_bytes=32 * 2**20),
         cost_estimate=pl.CostEstimate(
             flops=36 * 4 * 512 * 512 * HD,
             bytes_accessed=4 * 2**20,
@@ -229,44 +253,47 @@
 
 
 def merge_body(got_ref, mixed_ref, log_ref):
-    side = pl.program_id(0)
-    lane = lax.broadcasted_iota(jnp.int32, (64, HD), 1)
-    joints = []
-    for xh in range(2):
-        sums = []
-        for member in range(2):
-            stat = got_ref[member, xh, :, HELD * HD :].astype(jnp.float32)
-            sums.append(stat + pltpu.roll(stat, HD - 32, 1) + pltpu.roll(stat, HD - 64, 1))
-        high = jnp.maximum(sums[0], sums[1])
-        joint = high + jnp.log(jnp.exp(sums[0] - high) + jnp.exp(sums[1] - high))
-        joints.append(joint)
-        share = [jnp.exp(part - joint) for part in sums]
+    lower = lax.broadcasted_iota(jnp.int32, (8, HD), 0) < HELD
+    shares = []
+    for side in range(SIDES):
+        joints = []
+        for xh in range(2):
+            sums = []
+            for member in range(2):
+                terms = got_ref[member, side * 2 + xh, 64:, : 3 * HD].astype(jnp.float32)
+                sums.append(sum(columns(terms)))
+            high = jnp.maximum(sums[0], sums[1])
+            joint = high + jnp.log(jnp.exp(sums[0] - high) + jnp.exp(sums[1] - high))
+            joints.append(joint)
+            shares += [jnp.exp(part - joint) for part in sums]
+        logs = jnp.where(lower, joints[0], joints[1])
+        log_ref[side * GROUP : (side + 1) * GROUP, :] = logs[:, :64]
+    share = jnp.concatenate(shares, axis=0).T[:64, :]
+    for block in range(2 * SIDES):
         for head in range(HELD):
             cols = slice(head * HD, (head + 1) * HD)
-            into = slice((xh * HELD + head) * HD, (xh * HELD + head + 1) * HD)
-            mixed_ref[:, into] = (
-                got_ref[0, xh, :, cols].astype(jnp.float32) * share[0][:, head : head + 1]
-                + got_ref[1, xh, :, cols].astype(jnp.float32) * share[1][:, head : head + 1]
+            at = (block * HELD + head) * HD
+            first, second = block * 16 + head, block * 16 + 8 + head
+            mixed_ref[:, at : at + HD] = (
+                got_ref[0, block, :64, cols].astype(jnp.float32) * share[:, first : first + 1]
+                + got_ref[1, block, :64, cols].astype(jnp.float32)
+                * share[:, second : second + 1]
             ).astype(jnp.bfloat16)
-    logs = jnp.where(lane < HELD, joints[0], joints[1])
-    log_ref[pl.ds(pl.multiple_of(side * GROUP, GROUP), GROUP), :] = logs.T[:GROUP, :]
 
 
 def merge(got):
+    whole = pl.BlockSpec(memory_space=pltpu.VMEM)
     return pl.pallas_call(
         merge_body,
-        grid=(SIDES,),
         out_shape=(
             jax.ShapeDtypeStruct((64, HQ * HD), jnp.bfloat16),
             jax.ShapeDtypeStruct((HQ, 64), jnp.float32),
         ),
-        in_specs=[pl.BlockSpec((2, 2, 64, WIDE), lambda side: (0, side, 0, 0))],
-        out_specs=(
-            pl.BlockSpec((64, GROUP * HD), lambda side: (0, side)),
-            pl.BlockSpec((HQ, 64), lambda side: (0, 0)),
-        ),
+        in_specs=[whole],
+        out_specs=(whole, whole),
+        compiler_params=pltpu.CompilerParams(vmem_limit_bytes=8 * 2**20),
         name="merge",
-    )(got.reshape(2, 2 * SIDES, 64, WIDE))
+    )(got.reshape(2, 2 * SIDES, ROWS, HELD * HD))
 
 
 def per_device(queries, key_states, value_states):
@@ -276,7 +303,7 @@
 
     own = lax.all_to_all(
         pack(key_states, value_states), EVERY, 0, 0, axis_index_groups=KEY_GROUPS
-    ).reshape(8, 256, 2 * HD)
+    )
 
     by_shift = split(place, queries)
     q_pieces = []
@@ -288,7 +315,7 @@
                 piece = lax.ppermute(piece, EVERY, pairs)
             q_pieces.append(piece)
 
-    own, q_pieces = lax.optimization_barrier((own, q_pieces))
+    own, q_pieces[1:] = lax.optimization_barrier((own, q_pieces[1:]))
     other = lax.ppermute(own, EVERY, [(i, i ^ 1) for i in range(DEVICES)])
     partial = attend(place, q_pieces, own, other)
     got = lax.all_to_all(partial, EVERY, 0, 0, axis_index_groups=OUTPUT_GROUPS)

time: 84.1 us -> 76.7 us (0.912)
  Pallas kernels: 25.5 us -> 20.5 us
  blocking collectives: 29.8 us -> 27.8 us
  waiting for transfers between devices: 12.8 us -> 14.3 us
  local copies, waits for them, and re-layouts: 0.95 us -> 0.01 us
    pallas_call x2, Pallas kernels: 21.7 us -> 18 us  [the longest x1 16.3 us: attend(): pl.pallas_call(attend_body, out_shape=jax.ShapeDtypeStruct((16, ROWS, HEL...]
    all_to_all x1, blocking collectives: 29.8 us -> 27.8 us  [per_device(): got = lax.all_to_all(partial, EVERY, 0, 0, axis_index_groups=OUTPUT_GROUPS)]
    all_to_all x1, waiting for transfers between devices: 0.01 us -> 1.43 us  [per_device(): lax.all_to_all(pack(key_states, value_states), EVERY, 0, 0, axis_index_gr...]
    pallas_call x1, Pallas kernels: 1.88 us -> 0.58 us  [split(): pl.pallas_call(split_body, out_shape=[jax.ShapeDtypeStruct((8, 64, 2 * HD...]
    unnamed x4 -> x2, local copies, waits for them, and re-layouts: 0.95 us -> 0.01 us
  transfers between devices with their start and end apart: 5 -> 5, of which waited for: 3 -> 4; matrix products, arithmetic and copies ran while one was open for 1% -> 0% of each run, Pallas kernels for 2% -> 1%
where the time goes in v3:
time: 76.7 us; the launch traced here: 76.4 us
  blocking collectives  27.8 us (36%)
  Pallas kernels  20.5 us (27%)
  waiting for transfers between devices  14.3 us (19%)
  starting transfers between devices  13 us (17%)
    all_to_all x1, blocking collectives, per_device(): got = lax.all_to_all(partial, EVERY, 0, 0, axis_index_groups=OUTPUT_GROUPS)  27.8 us
    pallas_call x1, Pallas kernels, attend(): pl.pallas_call(attend_body, out_shape=jax.ShapeDtypeStruct((16, ROWS, HEL...  16.3 us
    ppermute x3, waiting for transfers between devices, per_device(): piece = lax.ppermute(piece, EVERY, pairs)  10.2 us
    all_to_all x1, starting transfers between devices, per_device(): lax.all_to_all(pack(key_states, value_states), EVERY, 0, 0, axis_index_gr...  9.61 us
    ppermute x3, starting transfers between devices, per_device(): piece = lax.ppermute(piece, EVERY, pairs)  3.43 us
    ppermute x1, waiting for transfers between devices, per_device(): other = lax.ppermute(own, EVERY, [(i, i ^ 1) for i in range(DEVICES)])  2.66 us
    pallas_call x1, Pallas kernels, pack(): pl.pallas_call(pack_body, out_shape=jax.ShapeDtypeStruct((32, 64, 2 * HD)...  1.98 us
    pallas_call x1, Pallas kernels, merge(): pl.pallas_call(merge_body, out_shape=(jax.ShapeDtypeStruct((64, HQ * HD),...  1.65 us
  transfers between devices with their start and end apart: 5, of which 4 were waited for; matrix products, arithmetic and copies ran while one was open for 0% of the time, Pallas kernels for 1%

profile of v3, /device:TPU:2, one launch (start us, length us, event | category | flops | bytes accessed | tf_op | source)
XLA Modules:
  0.0 76.4 jit_solution(700230398145590057)
XLA Ops:
  0.6 2.0 %pack.1 = bf16[32,64,256]{2,1,0:T(8,128)(2,1)} custom-call(bf16[64,512]{1,0:T(8,128)(2,1)} %key_ref.1, bf16[64,512]{1,0:T(8,128)(2,1)} %value_ref.1), custom_call_target="tpu_custom_call" | custom-call | tf_op jit(solution)/shard_map/pack/pallas_call | solution.py:63
  2.6 0.0 copy-start
  2.6 9.6 %all-to-all-start = ((bf16[32,64,256]{2,1,0:T(8,128)(2,1)}), bf16[32,64,256]{2,1,0:T(8,128)(2,1)S(1)}, u32[]{:S(2)}, u32[]{:S(2)}) async-start(bf16[32,64,256]{2,1,0:T(8,128)(2,1)} %pack.1), calls=%async_computation | async-start | bytes 2097152 | tf_op jit(solution)/shard_map/all_to_all | solution.py:304
  12.2 0.1 pad_add_fusion.place
  12.3 0.0 copy-done
  12.3 0.6 split.1
  12.9 3.0 %collective-permute-start.1 = (bf16[8,64,256]{2,1,0:T(8,128)(2,1)S(1)}, bf16[8,64,256]{2,1,0:T(8,128)(2,1)S(1)}, u32[]{:S(2)}, u32[]{:S(2)}) collective-permute-start(bf16[8,64,256]{2,1,0:T(8,128)(2,1)S(1)} %get-tuple-element.10.refs_0_), channel_id=1, source_target_pairs={{0,96},{1,97},{2,98},{3,99},{4,100},{5,101},{6,102},{7,103},{8,104... | collective-permute-start | bytes 786440 | tf_op jit(solution)/shard_map/ppermute | solution.py:315
  15.9 0.0 collective-permute-start.2
  15.9 0.4 collective-permute-start
  16.3 6.8 %collective-permute-done.1.refs_2_ = bf16[8,64,256]{2,1,0:T(8,128)(2,1)S(1)} collective-permute-done((bf16[8,64,256]{2,1,0:T(8,128)(2,1)S(1)}, bf16[8,64,256]{2,1,0:T(8,128)(2,1)S(1)}, u32[]{:S(2)}, u32[]{:S(2)}) %collective-permute-start.1) | collective-permute-done | bytes 262176 | tf_op jit(solution)/shard_map/ppermute | solution.py:315
  23.2 3.4 %collective-permute-done.2.refs_3_ = bf16[8,64,256]{2,1,0:T(8,128)(2,1)S(1)} collective-permute-done((bf16[8,64,256]{2,1,0:T(8,128)(2,1)S(1)}, bf16[8,64,256]{2,1,0:T(8,128)(2,1)S(1)}, u32[]{:S(2)}, u32[]{:S(2)}) %collective-permute-start.2) | collective-permute-done | bytes 262176 | tf_op jit(solution)/shard_map/ppermute | solution.py:315
  26.5 0.0 collective-permute-done.refs_1_
  26.5 1.4 %all-to-all-done.refs_4_ = bf16[32,64,256]{2,1,0:T(8,128)(2,1)S(1)} async-done(((bf16[32,64,256]{2,1,0:T(8,128)(2,1)}), bf16[32,64,256]{2,1,0:T(8,128)(2,1)S(1)}, u32[]{:S(2)}, u32[]{:S(2)}) %all-to-all-start) | async-done | bytes 1048608 | tf_op jit(solution)/shard_map/all_to_all | solution.py:304
  28.0 0.0 collective-permute-start.3
  28.0 2.7 %collective-permute-done.3.refs_5_ = bf16[32,64,256]{2,1,0:T(8,128)(2,1)S(1)} collective-permute-done((bf16[32,64,256]{2,1,0:T(8,128)(2,1)S(1)}, bf16[32,64,256]{2,1,0:T(8,128)(2,1)S(1)}, u32[]{:S(2)}, u32[]{:S(2)}) %collective-permute-start.3) | collective-permute-done | bytes 1048608 | tf_op jit(solution)/shard_map/ppermute | solution.py:319
  30.6 16.3 %attend.1 = bf16[16,72,512]{2,1,0:T(8,128)(2,1)S(1)} custom-call(s32[2]{0:T(128)S(1)} %pad_add_fusion.place, bf16[8,64,256]{2,1,0:T(8,128)(2,1)S(1)} %get-tuple-element.10.refs_0_, bf16[8,64,256]{2,1,0:T(8,128)(2,1)S(1)} %collective-permute-done.refs_1_, bf16[8,64,256]{2,1,0:T(8,128)(2,1)S(1)} %collective-permute-done.1.refs_2_, ...), custom_call_target="tpu_custom_call" | custom-call | flops 4831838208 | bytes 4194304 | tf_op jit(solution)/shard_map/attend/pallas_call | solution.py:233
  47.0 27.8 %all_to_all.10 = bf16[16,72,512]{2,1,0:T(8,128)(2,1)S(1)} all-to-all(bf16[16,72,512]{2,1,0:T(8,128)(2,1)S(1)} %attend.1), channel_id=1, replica_groups={{0,2,4,6,8,10,12,14,96,98,100,102,104,106,108,110},{1,3,5,7,9,11,13,15,..., dimensions={0} | all-to-all | bytes 2359296 | tf_op jit(solution)/shard_map/all_to_all | solution.py:321
  74.8 1.6 %merge.1 = (bf16[64,4096]{1,0:T(8,128)(2,1)}, f32[32,64]{1,0:T(8,128)}) custom-call(bf16[2,8,72,512]{3,2,1,0:T(8,128)(2,1)S(1)} %bitcast.4), custom_call_target="tpu_custom_call" | custom-call | tf_op jit(solution)/shard_map/merge/pallas_call | solution.py:286
Async XLA Ops:
  2.6 9.7 %copy-start = (bf16[1024,256]{1,0:T(8,128)(2,1)S(1)}, bf16[1024,256]{1,0:T(8,128)(2,1)}, u32[]{:S(2)}) copy-start(bf16[1024,256]{1,0:T(8,128)(2,1)} %q_ref.1) | copy-start | bytes 1572868
  2.6 25.4 %all-to-all-start = ((bf16[32,64,256]{2,1,0:T(8,128)(2,1)}), bf16[32,64,256]{2,1,0:T(8,128)(2,1)S(1)}, u32[]{:S(2)}, u32[]{:S(2)}) async-start(bf16[32,64,256]{2,1,0:T(8,128)(2,1)} %pack.1), calls=%async_computation | async-start | bytes 2097152 | tf_op jit(solution)/shard_map/all_to_all | solution.py:304
  12.9 10.3 %collective-permute-start.1 = (bf16[8,64,256]{2,1,0:T(8,128)(2,1)S(1)}, bf16[8,64,256]{2,1,0:T(8,128)(2,1)S(1)}, u32[]{:S(2)}, u32[]{:S(2)}) collective-permute-start(bf16[8,64,256]{2,1,0:T(8,128)(2,1)S(1)} %get-tuple-element.10.refs_0_), channel_id=1, source_target_pairs={{0,96},{1,97},{2,98},{3,99},{4,100},{5,101},{6,102},{7,103},{8,104... | collective-permute-start | bytes 786440 | tf_op jit(solution)/shard_map/ppermute | solution.py:315
  15.9 10.6 %collective-permute-start.2 = (bf16[8,64,256]{2,1,0:T(8,128)(2,1)S(1)}, bf16[8,64,256]{2,1,0:T(8,128)(2,1)S(1)}, u32[]{:S(2)}, u32[]{:S(2)}) collective-permute-start(bf16[8,64,256]{2,1,0:T(8,128)(2,1)S(1)} %get-tuple-element.11), channel_id=1, source_target_pairs={{0,97},{1,96},{2,99},{3,98},{4,101},{5,100},{6,103},{7,102},{8,105... | collective-permute-start | bytes 786440 | tf_op jit(solution)/shard_map/ppermute | solution.py:315
  15.9 10.6 %collective-permute-start = (bf16[8,64,256]{2,1,0:T(8,128)(2,1)S(1)}, bf16[8,64,256]{2,1,0:T(8,128)(2,1)S(1)}, u32[]{:S(2)}, u32[]{:S(2)}) collective-permute-start(bf16[8,64,256]{2,1,0:T(8,128)(2,1)S(1)} %get-tuple-element.11), channel_id=1, source_target_pairs={{0,1},{1,0},{2,3},{3,2},{4,5},{5,4},{6,7},{7,6},{8,9},{9,8},{10,11... | collective-permute-start | bytes 786440 | tf_op jit(solution)/shard_map/ppermute | solution.py:315
  28.0 2.7 %collective-permute-start.3 = (bf16[32,64,256]{2,1,0:T(8,128)(2,1)S(1)}, bf16[32,64,256]{2,1,0:T(8,128)(2,1)S(1)}, u32[]{:S(2)}, u32[]{:S(2)}) collective-permute-start(bf16[32,64,256]{2,1,0:T(8,128)(2,1)S(1)} %all-to-all-done.refs_4_), channel_id=1, source_target_pairs={{0,1},{1,0},{2,3},{3,2},{4,5},{5,4},{6,7},{7,6},{8,9},{9,8},{10,11... | collective-permute-start | bytes 3145736 | tf_op jit(solution)/shard_map/ppermute | solution.py:319

commit v4 on v3

v4 whole, which is shorter than its diff:
```python
import functools
import math

import jax
import jax.numpy as jnp
from jax import lax
from jax.experimental import pallas as pl
from jax.experimental.pallas import tpu as pltpu
from jax.sharding import PartitionSpec as P

HQ = 32
KVH = 4
HD = 128
GROUP = 8
EVERY = ("qrow", "kcol")
SPANS = 8
DEVICES = 128
SIDES = 4

NEG_FILL = -1e30
LOG2E = math.log2(math.e)
LN2 = math.log(2.0)
HELD = 4
DEPTH = 136


def device_at(span, side, slot):
    return span * 16 + side * 4 + slot


KEY_GROUPS = [
    [
        device_at(half * 4 + near, side, xh * 2 + core)
        for near in range(4)
        for xh in range(2)
        for side in range(SIDES)
    ]
    for half in range(2)
    for core in range(2)
]
OUTPUT_GROUPS = [
    [
        device_at(span, side, xh * 2 + core)
        for span in (low, low ^ 6)
        for side in range(SIDES)
        for xh in range(2)
    ]
    for low in range(SPANS // 2)
    for core in range(2)
]


def pack_body(key_ref, value_ref, out_ref):
    for side in range(SIDES):
        cols = slice(side * HD, (side + 1) * HD)
        for copy in range(8):
            out_ref[copy * SIDES + side, :, :HD] = key_ref[:, cols]
            out_ref[copy * SIDES + side, :, HD:] = value_ref[:, cols]


def pack(key_states, value_states):
    whole = pl.BlockSpec(memory_space=pltpu.VMEM)
    return pl.pallas_call(
        pack_body,
        out_shape=jax.ShapeDtypeStruct((32, 64, 2 * HD), jnp.bfloat16),
        in_specs=[whole, whole],
        out_specs=whole,
        name="pack",
    )(key_states, value_states)


def split_body(place, q_ref, *out_refs):
    core = place[1] & 1
    for shift in range(2):
        for piece in range(8):
            at = pl.multiple_of(piece * 128 + (core ^ shift) * 64, 64)
            out_refs[shift][piece] = q_ref[pl.ds(at, 64), :]


def split(place, queries):
    whole = pl.BlockSpec(memory_space=pltpu.VMEM)
    return pl.pallas_call(
        split_body,
        out_shape=[jax.ShapeDtypeStruct((8, 64, 2 * HD), jnp.bfloat16)] * 2,
        in_specs=[pl.BlockSpec(memory_space=pltpu.SMEM), whole],
        out_specs=[whole] * 2,
        cost_estimate=pl.CostEstimate(
            flops=2 * 10**10, bytes_accessed=2**20, transcendentals=0
        ),
        compiler_params=pltpu.CompilerParams(vmem_limit_bytes=8 * 2**20),
        name="split",
    )(place, queries)


def grouped(scores):
    return scores.reshape(scores.shape[0] // 8, 8, scores.shape[1])


def highest(parts):
    high = functools.reduce(jnp.maximum, [jnp.max(grouped(part), axis=0) for part in parts])
    return jnp.broadcast_to(jnp.max(high, axis=0, keepdims=True), high.shape)


def exponentials(parts, peak):
    return [
        jnp.exp2(grouped(part) - peak[None]).reshape(part.shape) for part in parts
    ]


def summed(parts):
    return functools.reduce(jnp.add, [jnp.sum(grouped(part), axis=0) for part in parts])


def attend_body(place, *refs):
    q_refs = refs[:4]
    own_ref, other_ref, o_ref, q_all, keys, values, acc, top, total, key_size, safe_now = refs[4:]
    row, column = place[0], place[1]
    half, core = row >> 2, column & 1

    for ref, part in ((own_ref, core), (other_ref, 1 - core)):
        for block in range(8):
            side, xh = block // 2, block % 2
            for near in range(4):
                held = pl.ds(pl.multiple_of(part * 256 + near * 64, 64), 64)
                piece = (near * 2 + xh) * SIDES + side
                keys[block, held, :] = ref[piece, :, :HD]
                values[block, held, :] = ref[piece, :, HD:]

    def lengths(vectors):
        return lax.dot_general(
            jnp.ones((8, HD), jnp.bfloat16),
            vectors * vectors,
            (((1,), (1,)), ((), ())),
            preferred_element_type=jnp.float32,
        )

    for block in range(7):
        key_size[block] = lengths(keys[block])

    def score(tile, block, width):
        return lax.dot_general(
            keys[block, :width, :],
            q_all[tile * 512 : (tile + 1) * 512, :],
            (((1,), (1,)), ((), ())),
            preferred_element_type=jnp.float32,
        ) * (LOG2E / math.sqrt(HD))

    def gathered(blocks, weights):
        return sum(
            lax.dot_general(
                values[block, : weight.shape[0], :],
                weight.astype(jnp.bfloat16),
                (((0,), (0,)), ((), ())),
                preferred_element_type=jnp.float32,
            )
            for block, weight in zip(blocks, weights)
        )

    def weigh(tile, parts):
        old = top[tile]
        new = jnp.maximum(old, highest(parts))
        scale = jnp.exp2(old - new)
        weights = exponentials(parts, new)
        top[tile] = new
        total[tile] = total[tile] * scale + summed(weights)
        return weights, scale

    def add(tile, blocks, weights, scale):
        acc[tile] = acc[tile] * scale[:1] + gathered(blocks, weights)

    in_key = lax.broadcasted_iota(jnp.int32, (256, 512), 0)
    in_tile = lax.broadcasted_iota(jnp.int32, (256, 512), 1)
    in_row = (in_tile >> 8) * 128 + (in_tile & 63)
    for turn in range(2):
        span = row if turn == 0 else row ^ 6
        member = (row >> 2) ^ turn
        for shift in range(2):
            for piece in range(8):
                for head in range(2):
                    at = piece * 256 + (core ^ shift) * 128 + head * 64
                    q_all[pl.ds(pl.multiple_of(at, 64), 64), :] = q_refs[turn * 2 + shift][
                        piece, :, head * HD : (head + 1) * HD
                    ]

        def ahead(tile):
            return score(tile, span, 256 if tile < 2 else 512)

        ready = ahead(0)
        for tile in range(4):
            later = ahead(tile + 1) if tile < 3 else None
            edge, parts = ready[-256:], [ready[:256]] if tile >= 2 else []
            reach = in_row + (tile % 2) * 256 + core * 64 - half * 256
            keep = in_key <= reach
            edge = jnp.where(keep, edge, NEG_FILL)
            peak = highest(parts + [edge])
            weights = exponentials(parts, peak)
            weights.append(jnp.where(keep, exponentials([edge], peak)[0], 0.0))
            top[tile] = peak
            total[tile] = summed(weights)
            acc[tile] = gathered([span], [jnp.concatenate(weights, axis=0)])
            ready = later

        longest = jnp.zeros((8, 512), jnp.float32)
        for block in range(7):
            longest = jnp.maximum(longest, jnp.where(block < span, key_size[block], 0.0))
        longest = jnp.max(longest)

        def settle():
            over, held = [], []
            for tile in range(4):
                squares = lengths(q_all[tile * 512 : (tile + 1) * 512, :])
                bound = jnp.sqrt(squares * longest) * (1.02 * LOG2E / math.sqrt(HD))
                held.append(jnp.where(top[tile] > 0.5 * NEG_FILL, top[tile], 0.0))
                over.append(bound - held[tile])
            calm = jnp.max(functools.reduce(jnp.maximum, over)) <= 100.0
            safe_now[0] = calm.astype(jnp.int32)

            @pl.when(calm)
            def _():
                for tile in range(4):
                    top[tile] = held[tile]

        settle()

        def sweep(blocks):
            units = [(tile, block, at) for block in blocks for tile in range(4) for at in range(0, 512, 512)]

            def unit_score(unit):
                tile, block, at = unit
                return lax.dot_general(
                    keys[block, at : at + 512, :],
                    q_all[tile * 512 : (tile + 1) * 512, :],
                    (((1,), (1,)), ((), ())),
                    preferred_element_type=jnp.float32,
                ) * (LOG2E / math.sqrt(HD))

            def unit_add(unit, weight):
                tile, block, at = unit
                acc[tile] += lax.dot_general(
                    values[block, at : at + 512, :],
                    weight,
                    (((0,), (0,)), ((), ())),
                    preferred_element_type=jnp.float32,
                )

            ready, waiting = unit_score(units[0]), None
            for index, unit in enumerate(units):
                later = unit_score(units[index + 1]) if index + 1 < len(units) else None
                weight = exponentials([ready], top[unit[0]])[0]
                total[unit[0]] += summed([weight])
                if waiting is not None:
                    unit_add(units[index - 1], waiting)
                waiting, ready = weight.astype(jnp.bfloat16), later
            unit_add(units[-1], waiting)

        def exact_sweep(block):
            for tile in range(4):
                weights, scale = weigh(tile, [score(tile, block, 512)])
                add(tile, [block], weights, scale)

        @pl.loop(0, span // 2)
        def _(group):
            calm = safe_now[0]

            @pl.when(calm == 1)
            def _():
                sweep([group * 2 + i for i in range(2)])

            @pl.when(calm == 0)
            def _():
                for i in range(2):
                    exact_sweep(group * 2 + i)
                settle()

        @pl.when((span & 1) == 1)
        def _():
            calm = safe_now[0]

            @pl.when(calm == 1)
            def _():
                sweep([span - 1])

            @pl.when(calm == 0)
            def _():
                exact_sweep(span - 1)

        term = lax.broadcasted_iota(jnp.int32, (8, 512), 0)
        for tile in range(4):
            whole = jnp.sum(total[tile], axis=0, keepdims=True)
            some = whole > 0
            safe = jnp.where(some, whole, 1.0)
            normed = (acc[tile] * (1.0 / safe)).astype(jnp.bfloat16)
            stat = jnp.where(some, (top[tile] + jnp.log2(safe)) * LN2, NEG_FILL)
            coarse = stat.astype(jnp.bfloat16).astype(jnp.float32)
            middle = (stat - coarse).astype(jnp.bfloat16).astype(jnp.float32)
            fine = stat - coarse - middle
            terms = jnp.where(term == 0, coarse, jnp.where(term == 1, middle, fine))
            for part in range(2):
                cols = slice(part * 256, (part + 1) * 256)
                at = member * 8 + tile * 2 + part
                o_ref[at, :HD, :] = normed[:, cols]
                o_ref[at, HD:, :] = terms[:, cols].astype(jnp.bfloat16)


def attend(place, q_pieces, own, other):
    whole = pl.BlockSpec(memory_space=pltpu.VMEM)
    return pl.pallas_call(
        attend_body,
        out_shape=jax.ShapeDtypeStruct((16, DEPTH, 256), jnp.bfloat16),
        in_specs=[pl.BlockSpec(memory_space=pltpu.SMEM)] + [whole] * 6,
        out_specs=whole,
        scratch_shapes=[
            pltpu.VMEM((2048, HD), jnp.bfloat16),
            pltpu.VMEM((8, 512, HD), jnp.bfloat16),
            pltpu.VMEM((8, 512, HD), jnp.bfloat16),
            pltpu.VMEM((4, HD, 512), jnp.float32),
            pltpu.VMEM((4, 8, 512), jnp.float32),
            pltpu.VMEM((4, 8, 512), jnp.float32),
            pltpu.VMEM((7, 8, 512), jnp.float32),
            pltpu.SMEM((1,), jnp.int32),
        ],
        compiler_params=pltpu.CompilerParams(vmem_limit_bytes=32 * 2**20),
        cost_estimate=pl.CostEstimate(
            flops=36 * 4 * 512 * 512 * HD,
            bytes_accessed=4 * 2**20,
            transcendentals=36 * 512 * 512,
        ),
        name="attend",
    )(place, *q_pieces, own, other)


def merge_body(got_ref, mixed_ref, log_ref):
    for block in range(2 * SIDES):
        sums = []
        for member in range(2):
            terms = got_ref[member, block, HD:, :].astype(jnp.float32)
            sums.append(terms[0:1] + terms[1:2] + terms[2:3])
        high = jnp.maximum(sums[0], sums[1])
        joint = high + jnp.log(jnp.exp(sums[0] - high) + jnp.exp(sums[1] - high))
        mixed = got_ref[0, block, :HD, :].astype(jnp.float32) * jnp.exp(sums[0] - joint) + (
            got_ref[1, block, :HD, :].astype(jnp.float32) * jnp.exp(sums[1] - joint)
        )
        for pair in range(2):
            rows = mixed[:, pair * HD : (pair + 1) * HD].T.astype(jnp.bfloat16)
            for head in range(2):
                place = block * HELD + pair * 2 + head
                mixed_ref[:, place * HD : (place + 1) * HD] = rows[head * 64 : (head + 1) * 64]
                at = (pair * 2 + head) * 64
                log_ref[place : place + 1, :] = joint[:, at : at + 64]


def merge(got):
    whole = pl.BlockSpec(memory_space=pltpu.VMEM)
    return pl.pallas_call(
        merge_body,
        out_shape=(
            jax.ShapeDtypeStruct((64, HQ * HD), jnp.bfloat16),
            jax.ShapeDtypeStruct((HQ, 64), jnp.float32),
        ),
        in_specs=[whole],
        out_specs=(whole, whole),
        compiler_params=pltpu.CompilerParams(vmem_limit_bytes=8 * 2**20),
        name="merge",
    )(got.reshape(2, 2 * SIDES, DEPTH, 256))


def per_device(queries, key_states, value_states):
    row = lax.axis_index("qrow")
    column = lax.axis_index("kcol")
    place = jnp.stack([row, column])

    own = lax.all_to_all(
        pack(key_states, value_states), EVERY, 0, 0, axis_index_groups=KEY_GROUPS
    )

    by_shift = split(place, queries)
    q_pieces = []
    for turn in range(2):
        for shift in range(2):
            piece = by_shift[shift]
            if turn or shift:
                pairs = [(i, i ^ shift ^ (96 * turn)) for i in range(DEVICES)]
                piece = lax.ppermute(piece, EVERY, pairs)
            q_pieces.append(piece)

    own, q_pieces[1:] = lax.optimization_barrier((own, q_pieces[1:]))
    other = lax.ppermute(own, EVERY, [(i, i ^ 1) for i in range(DEVICES)])
    partial = attend(place, q_pieces, own, other)
    got = lax.all_to_all(partial, EVERY, 0, 0, axis_index_groups=OUTPUT_GROUPS)
    mixed, logs = merge(got)
    return (mixed, logs.T)


def solution(mesh):
    placed = (P("qrow", "kcol"), P(("kcol", "qrow"), None), P(("kcol", "qrow"), None))
    return jax.shard_map(
        per_device,
        mesh=mesh,
        in_specs=placed,
        out_specs=(P(("qrow", "kcol"), None), P(("qrow", "kcol"), None)),
        check_vma=False,
    )
```

time: 76.7 us -> 82.4 us (1.074)
  Pallas kernels: 20.5 us -> 26.7 us
    pallas_call x1, Pallas kernels: 16.3 us -> 22.9 us  [attend(): pl.pallas_call(attend_body, out_shape=jax.ShapeDtypeStruct((16, DEPTH, 25...]
where the time goes in v4:
time: 82.4 us; the launch traced here: 82.1 us
  blocking collectives  27.3 us (33%)
  Pallas kernels  26.7 us (32%)
  waiting for transfers between devices  14.3 us (17%)
  starting transfers between devices  13 us (16%)
    all_to_all x1, blocking collectives, per_device(): got = lax.all_to_all(partial, EVERY, 0, 0, axis_index_groups=OUTPUT_GROUPS)  27.3 us
    pallas_call x1, Pallas kernels, attend(): pl.pallas_call(attend_body, out_shape=jax.ShapeDtypeStruct((16, DEPTH, 25...  22.9 us
    ppermute x3, waiting for transfers between devices, per_device(): piece = lax.ppermute(piece, EVERY, pairs)  10.2 us
    all_to_all x1, starting transfers between devices, per_device(): lax.all_to_all(pack(key_states, value_states), EVERY, 0, 0, axis_index_gr...  9.61 us
    ppermute x3, starting transfers between devices, per_device(): piece = lax.ppermute(piece, EVERY, pairs)  3.43 us
    ppermute x1, waiting for transfers between devices, per_device(): other = lax.ppermute(own, EVERY, [(i, i ^ 1) for i in range(DEVICES)])  2.66 us
    pallas_call x1, Pallas kernels, pack(): pl.pallas_call(pack_body, out_shape=jax.ShapeDtypeStruct((32, 64, 2 * HD)...  1.98 us
  transfers between devices with their start and end apart: 5, of which 4 were waited for; matrix products, arithmetic and copies ran while one was open for 0% of the time, Pallas kernels for 1%

profile of v4, /device:TPU:2, one launch (start us, length us, event | category | flops | bytes accessed | tf_op | source)
XLA Modules:
  0.0 82.1 jit_solution(6359150789877823977)
XLA Ops:
  0.6 2.0 %pack.1 = bf16[32,64,256]{2,1,0:T(8,128)(2,1)} custom-call(bf16[64,512]{1,0:T(8,128)(2,1)} %key_ref.1, bf16[64,512]{1,0:T(8,128)(2,1)} %value_ref.1), custom_call_target="tpu_custom_call" | custom-call | tf_op jit(solution)/shard_map/pack/pallas_call | solution.py:63
  2.6 0.0 copy-start
  2.6 9.6 %all-to-all-start = ((bf16[32,64,256]{2,1,0:T(8,128)(2,1)}), bf16[32,64,256]{2,1,0:T(8,128)(2,1)S(1)}, u32[]{:S(2)}, u32[]{:S(2)}) async-start(bf16[32,64,256]{2,1,0:T(8,128)(2,1)} %pack.1), calls=%async_computation | async-start | bytes 2097152 | tf_op jit(solution)/shard_map/all_to_all | solution.py:372
  12.2 0.1 pad_add_fusion.place
  12.3 0.0 copy-done
  12.3 0.6 split.1
  12.9 3.0 %collective-permute-start.1 = (bf16[8,64,256]{2,1,0:T(8,128)(2,1)S(1)}, bf16[8,64,256]{2,1,0:T(8,128)(2,1)S(1)}, u32[]{:S(2)}, u32[]{:S(2)}) collective-permute-start(bf16[8,64,256]{2,1,0:T(8,128)(2,1)S(1)} %get-tuple-element.10.refs_0_), channel_id=1, source_target_pairs={{0,96},{1,97},{2,98},{3,99},{4,100},{5,101},{6,102},{7,103},{8,104... | collective-permute-start | bytes 786440 | tf_op jit(solution)/shard_map/ppermute | solution.py:383
  15.9 0.0 collective-permute-start.2
  15.9 0.4 collective-permute-start
  16.3 6.8 %collective-permute-done.1.refs_2_ = bf16[8,64,256]{2,1,0:T(8,128)(2,1)S(1)} collective-permute-done((bf16[8,64,256]{2,1,0:T(8,128)(2,1)S(1)}, bf16[8,64,256]{2,1,0:T(8,128)(2,1)S(1)}, u32[]{:S(2)}, u32[]{:S(2)}) %collective-permute-start.1) | collective-permute-done | bytes 262176 | tf_op jit(solution)/shard_map/ppermute | solution.py:383
  23.2 3.4 %collective-permute-done.2.refs_3_ = bf16[8,64,256]{2,1,0:T(8,128)(2,1)S(1)} collective-permute-done((bf16[8,64,256]{2,1,0:T(8,128)(2,1)S(1)}, bf16[8,64,256]{2,1,0:T(8,128)(2,1)S(1)}, u32[]{:S(2)}, u32[]{:S(2)}) %collective-permute-start.2) | collective-permute-done | bytes 262176 | tf_op jit(solution)/shard_map/ppermute | solution.py:383
  26.5 0.0 collective-permute-done.refs_1_
  26.5 1.4 %all-to-all-done.refs_4_ = bf16[32,64,256]{2,1,0:T(8,128)(2,1)S(1)} async-done(((bf16[32,64,256]{2,1,0:T(8,128)(2,1)}), bf16[32,64,256]{2,1,0:T(8,128)(2,1)S(1)}, u32[]{:S(2)}, u32[]{:S(2)}) %all-to-all-start) | async-done | bytes 1048608 | tf_op jit(solution)/shard_map/all_to_all | solution.py:372
  28.0 0.0 collective-permute-start.3
  28.0 2.7 %collective-permute-done.3.refs_5_ = bf16[32,64,256]{2,1,0:T(8,128)(2,1)S(1)} collective-permute-done((bf16[32,64,256]{2,1,0:T(8,128)(2,1)S(1)}, bf16[32,64,256]{2,1,0:T(8,128)(2,1)S(1)}, u32[]{:S(2)}, u32[]{:S(2)}) %collective-permute-start.3) | collective-permute-done | bytes 1048608 | tf_op jit(solution)/shard_map/ppermute | solution.py:387
  30.6 22.9 %attend.1 = bf16[16,136,256]{2,1,0:T(8,128)(2,1)S(1)} custom-call(s32[2]{0:T(128)S(1)} %pad_add_fusion.place, bf16[8,64,256]{2,1,0:T(8,128)(2,1)S(1)} %get-tuple-element.10.refs_0_, bf16[8,64,256]{2,1,0:T(8,128)(2,1)S(1)} %collective-permute-done.refs_1_, bf16[8,64,256]{2,1,0:T(8,128)(2,1)S(1)} %collective-permute-done.1.refs_2_, ...), custom_call_target="tpu_custom_call" | custom-call | flops 4831838208 | bytes 4194304 | tf_op jit(solution)/shard_map/attend/pallas_call | solution.py:307
  53.6 27.3 %all_to_all.10 = bf16[16,136,256]{2,1,0:T(8,128)(2,1)S(1)} all-to-all(bf16[16,136,256]{2,1,0:T(8,128)(2,1)S(1)} %attend.1), channel_id=1, replica_groups={{0,2,4,6,8,10,12,14,96,98,100,102,104,106,108,110},{1,3,5,7,9,11,13,15,..., dimensions={0} | all-to-all | bytes 2228224 | tf_op jit(solution)/shard_map/all_to_all | solution.py:389
  80.9 1.2 %merge.1 = (bf16[64,4096]{1,0:T(8,128)(2,1)}, f32[32,64]{1,0:T(8,128)}) custom-call(bf16[2,8,136,256]{3,2,1,0:T(8,128)(2,1)S(1)} %bitcast.4), custom_call_target="tpu_custom_call" | custom-call | tf_op jit(solution)/shard_map/merge/pallas_call | solution.py:354
Async XLA Ops:
  2.6 9.7 %copy-start = (bf16[1024,256]{1,0:T(8,128)(2,1)S(1)}, bf16[1024,256]{1,0:T(8,128)(2,1)}, u32[]{:S(2)}) copy-start(bf16[1024,256]{1,0:T(8,128)(2,1)} %q_ref.1) | copy-start | bytes 1572868
  2.6 25.4 %all-to-all-start = ((bf16[32,64,256]{2,1,0:T(8,128)(2,1)}), bf16[32,64,256]{2,1,0:T(8,128)(2,1)S(1)}, u32[]{:S(2)}, u32[]{:S(2)}) async-start(bf16[32,64,256]{2,1,0:T(8,128)(2,1)} %pack.1), calls=%async_computation | async-start | bytes 2097152 | tf_op jit(solution)/shard_map/all_to_all | solution.py:372
  12.9 10.3 %collective-permute-start.1 = (bf16[8,64,256]{2,1,0:T(8,128)(2,1)S(1)}, bf16[8,64,256]{2,1,0:T(8,128)(2,1)S(1)}, u32[]{:S(2)}, u32[]{:S(2)}) collective-permute-start(bf16[8,64,256]{2,1,0:T(8,128)(2,1)S(1)} %get-tuple-element.10.refs_0_), channel_id=1, source_target_pairs={{0,96},{1,97},{2,98},{3,99},{4,100},{5,101},{6,102},{7,103},{8,104... | collective-permute-start | bytes 786440 | tf_op jit(solution)/shard_map/ppermute | solution.py:383
  15.9 10.6 %collective-permute-start.2 = (bf16[8,64,256]{2,1,0:T(8,128)(2,1)S(1)}, bf16[8,64,256]{2,1,0:T(8,128)(2,1)S(1)}, u32[]{:S(2)}, u32[]{:S(2)}) collective-permute-start(bf16[8,64,256]{2,1,0:T(8,128)(2,1)S(1)} %get-tuple-element.11), channel_id=1, source_target_pairs={{0,97},{1,96},{2,99},{3,98},{4,101},{5,100},{6,103},{7,102},{8,105... | collective-permute-start | bytes 786440 | tf_op jit(solution)/shard_map/ppermute | solution.py:383
  15.9 10.6 %collective-permute-start = (bf16[8,64,256]{2,1,0:T(8,128)(2,1)S(1)}, bf16[8,64,256]{2,1,0:T(8,128)(2,1)S(1)}, u32[]{:S(2)}, u32[]{:S(2)}) collective-permute-start(bf16[8,64,256]{2,1,0:T(8,128)(2,1)S(1)} %get-tuple-element.11), channel_id=1, source_target_pairs={{0,1},{1,0},{2,3},{3,2},{4,5},{5,4},{6,7},{7,6},{8,9},{9,8},{10,11... | collective-permute-start | bytes 786440 | tf_op jit(solution)/shard_map/ppermute | solution.py:383
  28.0 2.7 %collective-permute-start.3 = (bf16[32,64,256]{2,1,0:T(8,128)(2,1)S(1)}, bf16[32,64,256]{2,1,0:T(8,128)(2,1)S(1)}, u32[]{:S(2)}, u32[]{:S(2)}) collective-permute-start(bf16[32,64,256]{2,1,0:T(8,128)(2,1)S(1)} %all-to-all-done.refs_4_), channel_id=1, source_target_pairs={{0,1},{1,0},{2,3},{3,2},{4,5},{5,4},{6,7},{7,6},{8,9},{9,8},{10,11... | collective-permute-start | bytes 3145736 | tf_op jit(solution)/shard_map/ppermute | solution.py:387

commit v5 on v4

--- a/solution.py
+++ b/solution.py
@@ -206,19 +206,30 @@
         longest = jnp.max(longest)
 
         def settle():
-            over, held = [], []
+            fixed, width, lift = [], [], []
             for tile in range(4):
                 squares = lengths(q_all[tile * 512 : (tile + 1) * 512, :])
-                bound = jnp.sqrt(squares * longest) * (1.02 * LOG2E / math.sqrt(HD))
-                held.append(jnp.where(top[tile] > 0.5 * NEG_FILL, top[tile], 0.0))
-                over.append(bound - held[tile])
-            calm = jnp.max(functools.reduce(jnp.maximum, over)) <= 100.0
+                bound = jnp.sqrt(squares * longest) * (1.004 * LOG2E / math.sqrt(HD))
+                some = top[tile] > 0.5 * NEG_FILL
+                low = jnp.where(some, top[tile], -bound)
+                fixed.append(jnp.maximum(low, bound - 112.0))
+                width.append(bound - low)
+                lift.append(jnp.where(some, fixed[tile] - low, 0.0))
+            calm = jnp.max(functools.reduce(jnp.maximum, width)) <= 212.0
+            lifted = jnp.max(functools.reduce(jnp.maximum, lift)) > 0.0
             safe_now[0] = calm.astype(jnp.int32)
 
+            @pl.when(jnp.logical_and(calm, lifted))
+            def _():
+                for tile in range(4):
+                    scale = jnp.exp2(top[tile] - fixed[tile])
+                    total[tile] = total[tile] * scale
+                    acc[tile] = acc[tile] * scale[:1]
+
             @pl.when(calm)
             def _():
                 for tile in range(4):
-                    top[tile] = held[tile]
+                    top[tile] = fixed[tile]
 
         settle()
 

time: 82.4 us -> 82.4 us (level)
  no operation moved by 1% of the time
where the time goes in v5:
time: 82.4 us; the launch traced here: 82.1 us
  blocking collectives  27.3 us (33%)
  Pallas kernels  26.7 us (32%)
  waiting for transfers between devices  14.3 us (17%)
  starting transfers between devices  13 us (16%)
    all_to_all x1, blocking collectives, per_device(): got = lax.all_to_all(partial, EVERY, 0, 0, axis_index_groups=OUTPUT_GROUPS)  27.3 us
    pallas_call x1, Pallas kernels, attend(): pl.pallas_call(attend_body, out_shape=jax.ShapeDtypeStruct((16, DEPTH, 25...  22.9 us
    ppermute x3, waiting for transfers between devices, per_device(): piece = lax.ppermute(piece, EVERY, pairs)  10.2 us
    all_to_all x1, starting transfers between devices, per_device(): lax.all_to_all(pack(key_states, value_states), EVERY, 0, 0, axis_index_gr...  9.61 us
    ppermute x3, starting transfers between devices, per_device(): piece = lax.ppermute(piece, EVERY, pairs)  3.43 us
    ppermute x1, waiting for transfers between devices, per_device(): other = lax.ppermute(own, EVERY, [(i, i ^ 1) for i in range(DEVICES)])  2.66 us
    pallas_call x1, Pallas kernels, pack(): pl.pallas_call(pack_body, out_shape=jax.ShapeDtypeStruct((32, 64, 2 * HD)...  1.98 us
  transfers between devices with their start and end apart: 5, of which 4 were waited for; matrix products, arithmetic and copies ran while one was open for 0% of the time, Pallas kernels for 1%

profile of v5, /device:TPU:2, one launch (start us, length us, event | category | flops | bytes accessed | tf_op | source)
XLA Modules:
  0.0 82.1 jit_solution(16017701351840797518)
XLA Ops:
  0.6 2.0 %pack.1 = bf16[32,64,256]{2,1,0:T(8,128)(2,1)} custom-call(bf16[64,512]{1,0:T(8,128)(2,1)} %key_ref.1, bf16[64,512]{1,0:T(8,128)(2,1)} %value_ref.1), custom_call_target="tpu_custom_call" | custom-call | tf_op jit(solution)/shard_map/pack/pallas_call | solution.py:63
  2.6 0.0 copy-start
  2.6 9.6 %all-to-all-start = ((bf16[32,64,256]{2,1,0:T(8,128)(2,1)}), bf16[32,64,256]{2,1,0:T(8,128)(2,1)S(1)}, u32[]{:S(2)}, u32[]{:S(2)}) async-start(bf16[32,64,256]{2,1,0:T(8,128)(2,1)} %pack.1), calls=%async_computation | async-start | bytes 2097152 | tf_op jit(solution)/shard_map/all_to_all | solution.py:383
  12.2 0.1 pad_add_fusion.place
  12.3 0.0 copy-done
  12.3 0.6 split.1
  12.9 3.0 %collective-permute-start.1 = (bf16[8,64,256]{2,1,0:T(8,128)(2,1)S(1)}, bf16[8,64,256]{2,1,0:T(8,128)(2,1)S(1)}, u32[]{:S(2)}, u32[]{:S(2)}) collective-permute-start(bf16[8,64,256]{2,1,0:T(8,128)(2,1)S(1)} %get-tuple-element.10.refs_0_), channel_id=1, source_target_pairs={{0,96},{1,97},{2,98},{3,99},{4,100},{5,101},{6,102},{7,103},{8,104... | collective-permute-start | bytes 786440 | tf_op jit(solution)/shard_map/ppermute | solution.py:394
  15.9 0.0 collective-permute-start.2
  15.9 0.4 collective-permute-start
  16.3 6.8 %collective-permute-done.1.refs_2_ = bf16[8,64,256]{2,1,0:T(8,128)(2,1)S(1)} collective-permute-done((bf16[8,64,256]{2,1,0:T(8,128)(2,1)S(1)}, bf16[8,64,256]{2,1,0:T(8,128)(2,1)S(1)}, u32[]{:S(2)}, u32[]{:S(2)}) %collective-permute-start.1) | collective-permute-done | bytes 262176 | tf_op jit(solution)/shard_map/ppermute | solution.py:394
  23.2 3.4 %collective-permute-done.2.refs_3_ = bf16[8,64,256]{2,1,0:T(8,128)(2,1)S(1)} collective-permute-done((bf16[8,64,256]{2,1,0:T(8,128)(2,1)S(1)}, bf16[8,64,256]{2,1,0:T(8,128)(2,1)S(1)}, u32[]{:S(2)}, u32[]{:S(2)}) %collective-permute-start.2) | collective-permute-done | bytes 262176 | tf_op jit(solution)/shard_map/ppermute | solution.py:394
  26.5 0.0 collective-permute-done.refs_1_
  26.5 1.4 %all-to-all-done.refs_4_ = bf16[32,64,256]{2,1,0:T(8,128)(2,1)S(1)} async-done(((bf16[32,64,256]{2,1,0:T(8,128)(2,1)}), bf16[32,64,256]{2,1,0:T(8,128)(2,1)S(1)}, u32[]{:S(2)}, u32[]{:S(2)}) %all-to-all-start) | async-done | bytes 1048608 | tf_op jit(solution)/shard_map/all_to_all | solution.py:383
  28.0 0.0 collective-permute-start.3
  28.0 2.7 %collective-permute-done.3.refs_5_ = bf16[32,64,256]{2,1,0:T(8,128)(2,1)S(1)} collective-permute-done((bf16[32,64,256]{2,1,0:T(8,128)(2,1)S(1)}, bf16[32,64,256]{2,1,0:T(8,128)(2,1)S(1)}, u32[]{:S(2)}, u32[]{:S(2)}) %collective-permute-start.3) | collective-permute-done | bytes 1048608 | tf_op jit(solution)/shard_map/ppermute | solution.py:398
  30.6 22.9 %attend.1 = bf16[16,136,256]{2,1,0:T(8,128)(2,1)S(1)} custom-call(s32[2]{0:T(128)S(1)} %pad_add_fusion.place, bf16[8,64,256]{2,1,0:T(8,128)(2,1)S(1)} %get-tuple-element.10.refs_0_, bf16[8,64,256]{2,1,0:T(8,128)(2,1)S(1)} %collective-permute-done.refs_1_, bf16[8,64,256]{2,1,0:T(8,128)(2,1)S(1)} %collective-permute-done.1.refs_2_, ...), custom_call_target="tpu_custom_call" | custom-call | flops 4831838208 | bytes 4194304 | tf_op jit(solution)/shard_map/attend/pallas_call | solution.py:318
  53.6 27.3 %all_to_all.10 = bf16[16,136,256]{2,1,0:T(8,128)(2,1)S(1)} all-to-all(bf16[16,136,256]{2,1,0:T(8,128)(2,1)S(1)} %attend.1), channel_id=1, replica_groups={{0,2,4,6,8,10,12,14,96,98,100,102,104,106,108,110},{1,3,5,7,9,11,13,15,..., dimensions={0} | all-to-all | bytes 2228224 | tf_op jit(solution)/shard_map/all_to_all | solution.py:400
  80.9 1.2 %merge.1 = (bf16[64,4096]{1,0:T(8,128)(2,1)}, f32[32,64]{1,0:T(8,128)}) custom-call(bf16[2,8,136,256]{3,2,1,0:T(8,128)(2,1)S(1)} %bitcast.4), custom_call_target="tpu_custom_call" | custom-call | tf_op jit(solution)/shard_map/merge/pallas_call | solution.py:365
Async XLA Ops:
  2.6 9.7 %copy-start = (bf16[1024,256]{1,0:T(8,128)(2,1)S(1)}, bf16[1024,256]{1,0:T(8,128)(2,1)}, u32[]{:S(2)}) copy-start(bf16[1024,256]{1,0:T(8,128)(2,1)} %q_ref.1) | copy-start | bytes 1572868
  2.6 25.4 %all-to-all-start = ((bf16[32,64,256]{2,1,0:T(8,128)(2,1)}), bf16[32,64,256]{2,1,0:T(8,128)(2,1)S(1)}, u32[]{:S(2)}, u32[]{:S(2)}) async-start(bf16[32,64,256]{2,1,0:T(8,128)(2,1)} %pack.1), calls=%async_computation | async-start | bytes 2097152 | tf_op jit(solution)/shard_map/all_to_all | solution.py:383
  12.9 10.3 %collective-permute-start.1 = (bf16[8,64,256]{2,1,0:T(8,128)(2,1)S(1)}, bf16[8,64,256]{2,1,0:T(8,128)(2,1)S(1)}, u32[]{:S(2)}, u32[]{:S(2)}) collective-permute-start(bf16[8,64,256]{2,1,0:T(8,128)(2,1)S(1)} %get-tuple-element.10.refs_0_), channel_id=1, source_target_pairs={{0,96},{1,97},{2,98},{3,99},{4,100},{5,101},{6,102},{7,103},{8,104... | collective-permute-start | bytes 786440 | tf_op jit(solution)/shard_map/ppermute | solution.py:394
  15.9 10.6 %collective-permute-start.2 = (bf16[8,64,256]{2,1,0:T(8,128)(2,1)S(1)}, bf16[8,64,256]{2,1,0:T(8,128)(2,1)S(1)}, u32[]{:S(2)}, u32[]{:S(2)}) collective-permute-start(bf16[8,64,256]{2,1,0:T(8,128)(2,1)S(1)} %get-tuple-element.11), channel_id=1, source_target_pairs={{0,97},{1,96},{2,99},{3,98},{4,101},{5,100},{6,103},{7,102},{8,105... | collective-permute-start | bytes 786440 | tf_op jit(solution)/shard_map/ppermute | solution.py:394
  15.9 10.6 %collective-permute-start = (bf16[8,64,256]{2,1,0:T(8,128)(2,1)S(1)}, bf16[8,64,256]{2,1,0:T(8,128)(2,1)S(1)}, u32[]{:S(2)}, u32[]{:S(2)}) collective-permute-start(bf16[8,64,256]{2,1,0:T(8,128)(2,1)S(1)} %get-tuple-element.11), channel_id=1, source_target_pairs={{0,1},{1,0},{2,3},{3,2},{4,5},{5,4},{6,7},{7,6},{8,9},{9,8},{10,11... | collective-permute-start | bytes 786440 | tf_op jit(solution)/shard_map/ppermute | solution.py:394
  28.0 2.7 %collective-permute-start.3 = (bf16[32,64,256]{2,1,0:T(8,128)(2,1)S(1)}, bf16[32,64,256]{2,1,0:T(8,128)(2,1)S(1)}, u32[]{:S(2)}, u32[]{:S(2)}) collective-permute-start(bf16[32,64,256]{2,1,0:T(8,128)(2,1)S(1)} %all-to-all-done.refs_4_), channel_id=1, source_target_pairs={{0,1},{1,0},{2,3},{3,2},{4,5},{5,4},{6,7},{7,6},{8,9},{9,8},{10,11... | collective-permute-start | bytes 3145736 | tf_op jit(solution)/shard_map/ppermute | solution.py:398

commit v6 on v5

--- a/solution.py
+++ b/solution.py
@@ -50,6 +50,10 @@
 ]
 
 
+def swapped(array, bits):
+    return lax.ppermute(array, EVERY, [(i, i ^ bits) for i in range(DEVICES)])
+
+
 def pack_body(key_ref, value_ref, out_ref):
     for side in range(SIDES):
         cols = slice(side * HD, (side + 1) * HD)
@@ -69,27 +73,28 @@
     )(key_states, value_states)
 
 
-def split_body(place, q_ref, *out_refs):
+def split_body(place, own_ref, couple_ref, kept_ref, given_ref):
     core = place[1] & 1
-    for shift in range(2):
-        for piece in range(8):
-            at = pl.multiple_of(piece * 128 + (core ^ shift) * 64, 64)
-            out_refs[shift][piece] = q_ref[pl.ds(at, 64), :]
-
-
-def split(place, queries):
+    for shift, out_ref in ((0, kept_ref), (1, given_ref)):
+        for turn, ref in enumerate((own_ref, couple_ref)):
+            for piece in range(8):
+                at = pl.multiple_of(piece * 128 + (core ^ shift) * 64, 64)
+                out_ref[turn, piece] = ref[pl.ds(at, 64), :]
+
+
+def split(place, own, couple):
     whole = pl.BlockSpec(memory_space=pltpu.VMEM)
     return pl.pallas_call(
         split_body,
-        out_shape=[jax.ShapeDtypeStruct((8, 64, 2 * HD), jnp.bfloat16)] * 2,
-        in_specs=[pl.BlockSpec(memory_space=pltpu.SMEM), whole],
+        out_shape=[jax.ShapeDtypeStruct((2, 8, 64, 2 * HD), jnp.bfloat16)] * 2,
+        in_specs=[pl.BlockSpec(memory_space=pltpu.SMEM), whole, whole],
         out_specs=[whole] * 2,
         cost_estimate=pl.CostEstimate(
-            flops=2 * 10**10, bytes_accessed=2**20, transcendentals=0
+            flops=2 * 10**10, bytes_accessed=2**21, transcendentals=0
         ),
         compiler_params=pltpu.CompilerParams(vmem_limit_bytes=8 * 2**20),
         name="split",
-    )(place, queries)
+    )(place, own, couple)
 
 
 def grouped(scores):
@@ -112,8 +117,8 @@
 
 
 def attend_body(place, *refs):
-    q_refs = refs[:4]
-    own_ref, other_ref, o_ref, q_all, keys, values, acc, top, total, key_size, safe_now = refs[4:]
+    q_refs = refs[:2]
+    own_ref, other_ref, o_ref, q_all, keys, values, acc, top, total, key_size, safe_now = refs[2:]
     row, column = place[0], place[1]
     half, core = row >> 2, column & 1
 
@@ -178,8 +183,8 @@
             for piece in range(8):
                 for head in range(2):
                     at = piece * 256 + (core ^ shift) * 128 + head * 64
-                    q_all[pl.ds(pl.multiple_of(at, 64), 64), :] = q_refs[turn * 2 + shift][
-                        piece, :, head * HD : (head + 1) * HD
+                    q_all[pl.ds(pl.multiple_of(at, 64), 64), :] = q_refs[shift][
+                        turn, piece, :, head * HD : (head + 1) * HD
                     ]
 
         def ahead(tile):
@@ -318,7 +323,7 @@
     return pl.pallas_call(
         attend_body,
         out_shape=jax.ShapeDtypeStruct((16, DEPTH, 256), jnp.bfloat16),
-        in_specs=[pl.BlockSpec(memory_space=pltpu.SMEM)] + [whole] * 6,
+        in_specs=[pl.BlockSpec(memory_space=pltpu.SMEM)] + [whole] * 4,
         out_specs=whole,
         scratch_shapes=[
             pltpu.VMEM((2048, HD), jnp.bfloat16),
@@ -380,22 +385,17 @@
     column = lax.axis_index("kcol")
     place = jnp.stack([row, column])
 
+    couple = swapped(queries, 96)
     own = lax.all_to_all(
         pack(key_states, value_states), EVERY, 0, 0, axis_index_groups=KEY_GROUPS
     )
 
-    by_shift = split(place, queries)
-    q_pieces = []
-    for turn in range(2):
-        for shift in range(2):
-            piece = by_shift[shift]
-            if turn or shift:
-                pairs = [(i, i ^ shift ^ (96 * turn)) for i in range(DEVICES)]
-                piece = lax.ppermute(piece, EVERY, pairs)
-            q_pieces.append(piece)
-
-    own, q_pieces[1:] = lax.optimization_barrier((own, q_pieces[1:]))
-    other = lax.ppermute(own, EVERY, [(i, i ^ 1) for i in range(DEVICES)])
+    kept, given = split(place, queries, couple)
+    taken = swapped(given, 1)
+
+    own, taken = lax.optimization_barrier((own, taken))
+    q_pieces = [kept, taken]
+    other = swapped(own, 1)
     partial = attend(place, q_pieces, own, other)
     got = lax.all_to_all(partial, EVERY, 0, 0, axis_index_groups=OUTPUT_GROUPS)
     mixed, logs = merge(got)

time: 82.4 us -> 81.3 us (0.987)
  waiting for transfers between devices: 14.3 us -> 17.4 us
  blocking collectives: 27.3 us -> 24.3 us
  starting transfers between devices: 13 us -> 11.8 us
    all_to_all x1, waiting for transfers between devices: 1.43 us -> 13.3 us  [per_device(): lax.all_to_all(pack(key_states, value_states), EVERY, 0, 0, axis_index_gr...]
    ppermute x4 -> x3, waiting for transfers between devices: 12.9 us -> 4.13 us  [swapped(): return lax.ppermute(array, EVERY, [(i, i ^ bits) for i in range(DEVICES)])]
    all_to_all x1, blocking collectives: 27.3 us -> 24.3 us  [per_device(): got = lax.all_to_all(partial, EVERY, 0, 0, axis_index_groups=OUTPUT_GROUPS)]
    all_to_all x1, starting transfers between devices: 9.61 us -> 8.6 us  [per_device(): lax.all_to_all(pack(key_states, value_states), EVERY, 0, 0, axis_index_gr...]
    ppermute x4 -> x3, starting transfers between devices: 3.43 us -> 3.18 us  [swapped(): return lax.ppermute(array, EVERY, [(i, i ^ bits) for i in range(DEVICES)])]
  transfers between devices with their start and end apart: 5 -> 4, of which waited for: 4 -> 3; matrix products, arithmetic and copies ran while one was open for 0% -> 0% of each run, Pallas kernels for 1% -> 3%
where the time goes in v6:
time: 81.3 us; the launch traced here: 81 us
  Pallas kernels  26.7 us (33%)
  blocking collectives  24.3 us (30%)
  waiting for transfers between devices  17.4 us (21%)
  starting transfers between devices  11.8 us (15%)
    all_to_all x1, blocking collectives, per_device(): got = lax.all_to_all(partial, EVERY, 0, 0, axis_index_groups=OUTPUT_GROUPS)  24.3 us
    pallas_call x1, Pallas kernels, attend(): pl.pallas_call(attend_body, out_shape=jax.ShapeDtypeStruct((16, DEPTH, 25...  22.9 us
    all_to_all x1, waiting for transfers between devices, per_device(): lax.all_to_all(pack(key_states, value_states), EVERY, 0, 0, axis_index_gr...  13.3 us
    all_to_all x1, starting transfers between devices, per_device(): lax.all_to_all(pack(key_states, value_states), EVERY, 0, 0, axis_index_gr...  8.6 us
    ppermute x3, waiting for transfers between devices, swapped(): return lax.ppermute(array, EVERY, [(i, i ^ bits) for i in range(DEVICES)])  4.13 us
    ppermute x3, starting transfers between devices, swapped(): return lax.ppermute(array, EVERY, [(i, i ^ bits) for i in range(DEVICES)])  3.18 us
    pallas_call x1, Pallas kernels, pack(): pl.pallas_call(pack_body, out_shape=jax.ShapeDtypeStruct((32, 64, 2 * HD)...  1.97 us
  transfers between devices with their start and end apart: 4, of which 3 were waited for; matrix products, arithmetic and copies ran while one was open for 0% of the time, Pallas kernels for 3%

profile of v6, /device:TPU:2, one launch (start us, length us, event | category | flops | bytes accessed | tf_op | source)
XLA Modules:
  0.0 81.0 jit_solution(10610430973504366357)
XLA Ops:
  0.6 3.1 %collective-permute-start = (bf16[1024,256]{1,0:T(8,128)(2,1)}, bf16[1024,256]{1,0:T(8,128)(2,1)S(1)}, u32[]{:S(2)}, u32[]{:S(2)}) collective-permute-start(bf16[1024,256]{1,0:T(8,128)(2,1)} %own_ref.1), channel_id=1, source_target_pairs={{0,96},{1,97},{2,98},{3,99},{4,100},{5,101},{6,102},{7,103},{8,104... | collective-permute-start | bytes 1572872 | tf_op jit(solution)/shard_map/ppermute | solution.py:54
  3.7 2.0 %pack.1 = bf16[32,64,256]{2,1,0:T(8,128)(2,1)} custom-call(bf16[64,512]{1,0:T(8,128)(2,1)} %key_ref.1, bf16[64,512]{1,0:T(8,128)(2,1)} %value_ref.1), custom_call_target="tpu_custom_call" | custom-call | tf_op jit(solution)/shard_map/pack/pallas_call | solution.py:67
  5.7 0.0 copy-start
  5.7 8.6 %all-to-all-start = ((bf16[32,64,256]{2,1,0:T(8,128)(2,1)}), bf16[32,64,256]{2,1,0:T(8,128)(2,1)S(1)}, u32[]{:S(2)}, u32[]{:S(2)}) async-start(bf16[32,64,256]{2,1,0:T(8,128)(2,1)} %pack.1), calls=%async_computation | async-start | bytes 2097152 | tf_op jit(solution)/shard_map/all_to_all | solution.py:389
  14.3 0.1 pad_add_fusion.place
  14.4 1.5 %collective-permute-done.couple_ref = bf16[1024,256]{1,0:T(8,128)(2,1)S(1)} collective-permute-done((bf16[1024,256]{1,0:T(8,128)(2,1)}, bf16[1024,256]{1,0:T(8,128)(2,1)S(1)}, u32[]{:S(2)}, u32[]{:S(2)}) %collective-permute-start) | collective-permute-done | bytes 524320 | tf_op jit(solution)/shard_map/ppermute | solution.py:54
  15.9 0.0 copy-done
  15.9 0.6 split.1
  16.5 0.1 collective-permute-start.1
  16.6 13.3 %all-to-all-done.refs_2_ = bf16[32,64,256]{2,1,0:T(8,128)(2,1)S(1)} async-done(((bf16[32,64,256]{2,1,0:T(8,128)(2,1)}), bf16[32,64,256]{2,1,0:T(8,128)(2,1)S(1)}, u32[]{:S(2)}, u32[]{:S(2)}) %all-to-all-start) | async-done | bytes 1048608 | tf_op jit(solution)/shard_map/all_to_all | solution.py:389
  29.9 0.0 collective-permute-done.1.refs_1_
  29.9 0.0 collective-permute-start.2
  29.9 2.7 %collective-permute-done.2.refs_3_ = bf16[32,64,256]{2,1,0:T(8,128)(2,1)S(1)} collective-permute-done((bf16[32,64,256]{2,1,0:T(8,128)(2,1)S(1)}, bf16[32,64,256]{2,1,0:T(8,128)(2,1)S(1)}, u32[]{:S(2)}, u32[]{:S(2)}) %collective-permute-start.2) | collective-permute-done | bytes 1048608 | tf_op jit(solution)/shard_map/ppermute | solution.py:54
  32.5 22.9 %attend.1 = bf16[16,136,256]{2,1,0:T(8,128)(2,1)S(1)} custom-call(s32[2]{0:T(128)S(1)} %pad_add_fusion.place, bf16[2,8,64,256]{3,2,1,0:T(8,128)(2,1)S(1)} %get-tuple-element.8.refs_0_, bf16[2,8,64,256]{3,2,1,0:T(8,128)(2,1)S(1)} %collective-permute-done.1.refs_1_, bf16[32,64,256]{2,1,0:T(8,128)(2,1)S(1)} %all-to-all-done.refs_2_, ...), custom_call_target="tpu_custom_call" | custom-call | flops 4831838208 | bytes 4194304 | tf_op jit(solution)/shard_map/attend/pallas_call | solution.py:323
  55.5 24.3 %all_to_all.10 = bf16[16,136,256]{2,1,0:T(8,128)(2,1)S(1)} all-to-all(bf16[16,136,256]{2,1,0:T(8,128)(2,1)S(1)} %attend.1), channel_id=1, replica_groups={{0,2,4,6,8,10,12,14,96,98,100,102,104,106,108,110},{1,3,5,7,9,11,13,15,..., dimensions={0} | all-to-all | bytes 2228224 | tf_op jit(solution)/shard_map/all_to_all | solution.py:400
  79.8 1.2 %merge.1 = (bf16[64,4096]{1,0:T(8,128)(2,1)}, f32[32,64]{1,0:T(8,128)}) custom-call(bf16[2,8,136,256]{3,2,1,0:T(8,128)(2,1)S(1)} %bitcast.4), custom_call_target="tpu_custom_call" | custom-call | tf_op jit(solution)/shard_map/merge/pallas_call | solution.py:370
Async XLA Ops:
  0.6 15.2 %collective-permute-start = (bf16[1024,256]{1,0:T(8,128)(2,1)}, bf16[1024,256]{1,0:T(8,128)(2,1)S(1)}, u32[]{:S(2)}, u32[]{:S(2)}) collective-permute-start(bf16[1024,256]{1,0:T(8,128)(2,1)} %own_ref.1), channel_id=1, source_target_pairs={{0,96},{1,97},{2,98},{3,99},{4,100},{5,101},{6,102},{7,103},{8,104... | collective-permute-start | bytes 1572872 | tf_op jit(solution)/shard_map/ppermute | solution.py:54
  5.7 10.2 %copy-start = (bf16[1024,256]{1,0:T(8,128)(2,1)S(1)}, bf16[1024,256]{1,0:T(8,128)(2,1)}, u32[]{:S(2)}) copy-start(bf16[1024,256]{1,0:T(8,128)(2,1)} %own_ref.1) | copy-start | bytes 1572868
  5.7 24.2 %all-to-all-start = ((bf16[32,64,256]{2,1,0:T(8,128)(2,1)}), bf16[32,64,256]{2,1,0:T(8,128)(2,1)S(1)}, u32[]{:S(2)}, u32[]{:S(2)}) async-start(bf16[32,64,256]{2,1,0:T(8,128)(2,1)} %pack.1), calls=%async_computation | async-start | bytes 2097152 | tf_op jit(solution)/shard_map/all_to_all | solution.py:389
  16.5 13.4 %collective-permute-start.1 = (bf16[2,8,64,256]{3,2,1,0:T(8,128)(2,1)S(1)}, bf16[2,8,64,256]{3,2,1,0:T(8,128)(2,1)S(1)}, u32[]{:S(2)}, u32[]{:S(2)}) collective-permute-start(bf16[2,8,64,256]{3,2,1,0:T(8,128)(2,1)S(1)} %get-tuple-element.9), channel_id=1, source_target_pairs={{0,1},{1,0},{2,3},{3,2},{4,5},{5,4},{6,7},{7,6},{8,9},{9,8},{10,11... | collective-permute-start | bytes 1572872 | tf_op jit(solution)/shard_map/ppermute | solution.py:54
  29.9 2.7 %collective-permute-start.2 = (bf16[32,64,256]{2,1,0:T(8,128)(2,1)S(1)}, bf16[32,64,256]{2,1,0:T(8,128)(2,1)S(1)}, u32[]{:S(2)}, u32[]{:S(2)}) collective-permute-start(bf16[32,64,256]{2,1,0:T(8,128)(2,1)S(1)} %all-to-all-done.refs_2_), channel_id=1, source_target_pairs={{0,1},{1,0},{2,3},{3,2},{4,5},{5,4},{6,7},{7,6},{8,9},{9,8},{10,11... | collective-permute-start | bytes 3145736 | tf_op jit(solution)/shard_map/ppermute | solution.py:54

commit v7 on v6

--- a/solution.py
+++ b/solution.py
@@ -116,9 +116,47 @@
     return functools.reduce(jnp.add, [jnp.sum(grouped(part), axis=0) for part in parts])
 
 
+def lengths(vectors):
+    return lax.dot_general(
+        jnp.ones((8, HD), jnp.bfloat16),
+        vectors * vectors,
+        (((1,), (1,)), ((), ())),
+        preferred_element_type=jnp.float32,
+    )
+
+
+def arrange_body(place, kept_ref, taken_ref, q_both, q_size):
+    core = place[1] & 1
+    for turn in range(2):
+        for shift, ref in ((0, kept_ref), (1, taken_ref)):
+            for piece in range(8):
+                for head in range(2):
+                    at = piece * 256 + (core ^ shift) * 128 + head * 64
+                    q_both[turn, pl.ds(pl.multiple_of(at, 64), 64), :] = ref[
+                        turn, piece, :, head * HD : (head + 1) * HD
+                    ]
+        for tile in range(4):
+            q_size[turn, tile] = lengths(q_both[turn, tile * 512 : (tile + 1) * 512, :])
+
+
+def arrange(place, kept, taken):
+    whole = pl.BlockSpec(memory_space=pltpu.VMEM)
+    return pl.pallas_call(
+        arrange_body,
+        out_shape=[
+            jax.ShapeDtypeStruct((2, 2048, HD), jnp.bfloat16),
+            jax.ShapeDtypeStruct((2, 4, 8, 512), jnp.float32),
+        ],
+        in_specs=[pl.BlockSpec(memory_space=pltpu.SMEM), whole, whole],
+        out_specs=[whole, whole],
+        compiler_params=pltpu.CompilerParams(vmem_limit_bytes=8 * 2**20),
+        name="arrange",
+    )(place, kept, taken)
+
+
 def attend_body(place, *refs):
-    q_refs = refs[:2]
-    own_ref, other_ref, o_ref, q_all, keys, values, acc, top, total, key_size, safe_now = refs[2:]
+    q_both, q_size, own_ref, other_ref, o_ref = refs[:5]
+    keys, values, acc, top, total, key_size, safe_now = refs[5:]
     row, column = place[0], place[1]
     half, core = row >> 2, column & 1
 
@@ -131,18 +169,10 @@
                 keys[block, held, :] = ref[piece, :, :HD]
                 values[block, held, :] = ref[piece, :, HD:]
 
-    def lengths(vectors):
-        return lax.dot_general(
-            jnp.ones((8, HD), jnp.bfloat16),
-            vectors * vectors,
-            (((1,), (1,)), ((), ())),
-            preferred_element_type=jnp.float32,
-        )
-
     for block in range(7):
         key_size[block] = lengths(keys[block])
 
-    def score(tile, block, width):
+    def score(q_all, tile, block, width):
         return lax.dot_general(
             keys[block, :width, :],
             q_all[tile * 512 : (tile + 1) * 512, :],
@@ -179,16 +209,10 @@
     for turn in range(2):
         span = row if turn == 0 else row ^ 6
         member = (row >> 2) ^ turn
-        for shift in range(2):
-            for piece in range(8):
-                for head in range(2):
-                    at = piece * 256 + (core ^ shift) * 128 + head * 64
-                    q_all[pl.ds(pl.multiple_of(at, 64), 64), :] = q_refs[shift][
-                        turn, piece, :, head * HD : (head + 1) * HD
-                    ]
+        q_all = q_both.at[turn]
 
         def ahead(tile):
-            return score(tile, span, 256 if tile < 2 else 512)
+            return score(q_all, tile, span, 256 if tile < 2 else 512)
 
         ready = ahead(0)
         for tile in range(4):
@@ -213,8 +237,7 @@
         def settle():
             fixed, width, lift = [], [], []
             for tile in range(4):
-                squares = lengths(q_all[tile * 512 : (tile + 1) * 512, :])
-                bound = jnp.sqrt(squares * longest) * (1.004 * LOG2E / math.sqrt(HD))
+                bound = jnp.sqrt(q_size[turn, tile] * longest) * (1.004 * LOG2E / math.sqrt(HD))
                 some = top[tile] > 0.5 * NEG_FILL
                 low = jnp.where(some, top[tile], -bound)
                 fixed.append(jnp.maximum(low, bound - 112.0))
@@ -271,7 +294,7 @@
 
         def exact_sweep(block):
             for tile in range(4):
-                weights, scale = weigh(tile, [score(tile, block, 512)])
+                weights, scale = weigh(tile, [score(q_all, tile, block, 512)])
                 add(tile, [block], weights, scale)
 
         @pl.loop(0, span // 2)
@@ -326,7 +349,6 @@
         in_specs=[pl.BlockSpec(memory_space=pltpu.SMEM)] + [whole] * 4,
         out_specs=whole,
         scratch_shapes=[
-            pltpu.VMEM((2048, HD), jnp.bfloat16),
             pltpu.VMEM((8, 512, HD), jnp.bfloat16),
             pltpu.VMEM((8, 512, HD), jnp.bfloat16),
             pltpu.VMEM((4, HD, 512), jnp.float32),
@@ -393,10 +415,10 @@
     kept, given = split(place, queries, couple)
     taken = swapped(given, 1)
 
-    own, taken = lax.optimization_barrier((own, taken))
-    q_pieces = [kept, taken]
+    arranged = arrange(place, kept, taken)
+    own, arranged = lax.optimization_barrier((own, arranged))
     other = swapped(own, 1)
-    partial = attend(place, q_pieces, own, other)
+    partial = attend(place, arranged, own, other)
     got = lax.all_to_all(partial, EVERY, 0, 0, axis_index_groups=OUTPUT_GROUPS)
     mixed, logs = merge(got)
     return (mixed, logs.T)

time: 81.3 us -> 80 us (0.984)
  waiting for transfers between devices: 17.4 us -> 16.3 us
    all_to_all x1, waiting for transfers between devices: 13.3 us -> 10.3 us  [per_device(): lax.all_to_all(pack(key_states, value_states), EVERY, 0, 0, axis_index_gr...]
    ppermute x3, waiting for transfers between devices: 4.13 us -> 6.03 us  [swapped(): return lax.ppermute(array, EVERY, [(i, i ^ bits) for i in range(DEVICES)])]
    pallas_call x1, Pallas kernels: 22.9 us -> 21.7 us  [attend(): pl.pallas_call(attend_body, out_shape=jax.ShapeDtypeStruct((16, DEPTH, 25...]
    pallas_call x0 -> x1, Pallas kernels: none -> 1.1 us  [arrange(): pl.pallas_call(arrange_body, out_shape=[jax.ShapeDtypeStruct((2, 2048, HD...]
  transfers between devices with their start and end apart: 4 -> 4, of which waited for: 3 -> 4; matrix products, arithmetic and copies ran while one was open for 0% -> 0% of each run, Pallas kernels for 3% -> 5%
where the time goes in v7:
time: 80 us; the launch traced here: 79.7 us
  Pallas kernels  26.6 us (33%)
  blocking collectives  24.3 us (30%)
  waiting for transfers between devices  16.3 us (20%)
  starting transfers between devices  11.8 us (15%)
    all_to_all x1, blocking collectives, per_device(): got = lax.all_to_all(partial, EVERY, 0, 0, axis_index_groups=OUTPUT_GROUPS)  24.3 us
    pallas_call x1, Pallas kernels, attend(): pl.pallas_call(attend_body, out_shape=jax.ShapeDtypeStruct((16, DEPTH, 25...  21.7 us
    all_to_all x1, waiting for transfers between devices, per_device(): lax.all_to_all(pack(key_states, value_states), EVERY, 0, 0, axis_index_gr...  10.3 us
    all_to_all x1, starting transfers between devices, per_device(): lax.all_to_all(pack(key_states, value_states), EVERY, 0, 0, axis_index_gr...  8.6 us
    ppermute x3, waiting for transfers between devices, swapped(): return lax.ppermute(array, EVERY, [(i, i ^ bits) for i in range(DEVICES)])  6.03 us
    ppermute x3, starting transfers between devices, swapped(): return lax.ppermute(array, EVERY, [(i, i ^ bits) for i in range(DEVICES)])  3.18 us
    pallas_call x1, Pallas kernels, pack(): pl.pallas_call(pack_body, out_shape=jax.ShapeDtypeStruct((32, 64, 2 * HD)...  1.97 us
  transfers between devices with their start and end apart: 4, of which 4 were waited for; matrix products, arithmetic and copies ran while one was open for 0% of the time, Pallas kernels for 5%

profile of v7, /device:TPU:2, one launch (start us, length us, event | category | flops | bytes accessed | tf_op | source)
XLA Modules:
  0.0 79.7 jit_solution(15338503127955456453)
XLA Ops:
  0.6 3.1 %collective-permute-start = (bf16[1024,256]{1,0:T(8,128)(2,1)}, bf16[1024,256]{1,0:T(8,128)(2,1)S(1)}, u32[]{:S(2)}, u32[]{:S(2)}) collective-permute-start(bf16[1024,256]{1,0:T(8,128)(2,1)} %own_ref.1), channel_id=1, source_target_pairs={{0,96},{1,97},{2,98},{3,99},{4,100},{5,101},{6,102},{7,103},{8,104... | collective-permute-start | bytes 1572872 | tf_op jit(solution)/shard_map/ppermute | solution.py:54
  3.7 2.0 %pack.1 = bf16[32,64,256]{2,1,0:T(8,128)(2,1)} custom-call(bf16[64,512]{1,0:T(8,128)(2,1)} %key_ref.1, bf16[64,512]{1,0:T(8,128)(2,1)} %value_ref.1), custom_call_target="tpu_custom_call" | custom-call | tf_op jit(solution)/shard_map/pack/pallas_call | solution.py:67
  5.7 0.0 copy-start
  5.7 8.6 %all-to-all-start = ((bf16[32,64,256]{2,1,0:T(8,128)(2,1)}), bf16[32,64,256]{2,1,0:T(8,128)(2,1)S(1)}, u32[]{:S(2)}, u32[]{:S(2)}) async-start(bf16[32,64,256]{2,1,0:T(8,128)(2,1)} %pack.1), calls=%async_computation | async-start | bytes 2097152 | tf_op jit(solution)/shard_map/all_to_all | solution.py:411
  14.3 0.1 pad_add_fusion.place
  14.4 1.5 %collective-permute-done.couple_ref = bf16[1024,256]{1,0:T(8,128)(2,1)S(1)} collective-permute-done((bf16[1024,256]{1,0:T(8,128)(2,1)}, bf16[1024,256]{1,0:T(8,128)(2,1)S(1)}, u32[]{:S(2)}, u32[]{:S(2)}) %collective-permute-start) | collective-permute-done | bytes 524320 | tf_op jit(solution)/shard_map/ppermute | solution.py:54
  15.9 0.0 copy-done
  15.9 0.6 split.1
  16.5 0.1 collective-permute-start.1
  16.6 1.9 %collective-permute-done.1.taken_ref = bf16[2,8,64,256]{3,2,1,0:T(8,128)(2,1)S(1)} collective-permute-done((bf16[2,8,64,256]{3,2,1,0:T(8,128)(2,1)S(1)}, bf16[2,8,64,256]{3,2,1,0:T(8,128)(2,1)S(1)}, u32[]{:S(2)}, u32[]{:S(2)}) %collective-permute-start.1) | collective-permute-done | bytes 524320 | tf_op jit(solution)/shard_map/ppermute | solution.py:54
  18.5 1.1 %arrange.1 = (bf16[2,2048,128]{2,1,0:T(8,128)(2,1)S(1)}, f32[2,4,8,512]{3,2,1,0:T(8,128)S(1)}) custom-call(s32[2]{0:T(128)S(1)} %pad_add_fusion.place, bf16[2,8,64,256]{3,2,1,0:T(8,128)(2,1)S(1)} %get-tuple-element.11.kept_ref, bf16[2,8,64,256]{3,2,1,0:T(8,128)(2,1)S(1)} %collective-permute-done.1.taken_ref), custom_call_target="tpu_custom_call" | custom-call | tf_op jit(solution)/shard_map/arrange/pallas_call | solution.py:144
  19.6 10.3 %all-to-all-done.refs_2_ = bf16[32,64,256]{2,1,0:T(8,128)(2,1)S(1)} async-done(((bf16[32,64,256]{2,1,0:T(8,128)(2,1)}), bf16[32,64,256]{2,1,0:T(8,128)(2,1)S(1)}, u32[]{:S(2)}, u32[]{:S(2)}) %all-to-all-start) | async-done | bytes 1048608 | tf_op jit(solution)/shard_map/all_to_all | solution.py:411
  29.9 0.0 collective-permute-start.2
  29.9 2.7 %collective-permute-done.2.refs_3_ = bf16[32,64,256]{2,1,0:T(8,128)(2,1)S(1)} collective-permute-done((bf16[32,64,256]{2,1,0:T(8,128)(2,1)S(1)}, bf16[32,64,256]{2,1,0:T(8,128)(2,1)S(1)}, u32[]{:S(2)}, u32[]{:S(2)}) %collective-permute-start.2) | collective-permute-done | bytes 1048608 | tf_op jit(solution)/shard_map/ppermute | solution.py:54
  32.5 21.7 %attend.1 = bf16[16,136,256]{2,1,0:T(8,128)(2,1)S(1)} custom-call(s32[2]{0:T(128)S(1)} %pad_add_fusion.place, bf16[2,2048,128]{2,1,0:T(8,128)(2,1)S(1)} %get-tuple-element.15.refs_0_, f32[2,4,8,512]{3,2,1,0:T(8,128)S(1)} %get-tuple-element.16.refs_1_, bf16[32,64,256]{2,1,0:T(8,128)(2,1)S(1)} %all-to-all-done.refs_2_, ...), custom_call_target="tpu_custom_call" | custom-call | flops 4831838208 | bytes 4194304 | tf_op jit(solution)/shard_map/attend/pallas_call | solution.py:346
  54.3 24.3 %all_to_all.10 = bf16[16,136,256]{2,1,0:T(8,128)(2,1)S(1)} all-to-all(bf16[16,136,256]{2,1,0:T(8,128)(2,1)S(1)} %attend.1), channel_id=1, replica_groups={{0,2,4,6,8,10,12,14,96,98,100,102,104,106,108,110},{1,3,5,7,9,11,13,15,..., dimensions={0} | all-to-all | bytes 2228224 | tf_op jit(solution)/shard_map/all_to_all | solution.py:422
  78.5 1.2 %merge.1 = (bf16[64,4096]{1,0:T(8,128)(2,1)}, f32[32,64]{1,0:T(8,128)}) custom-call(bf16[2,8,136,256]{3,2,1,0:T(8,128)(2,1)S(1)} %bitcast.4), custom_call_target="tpu_custom_call" | custom-call | tf_op jit(solution)/shard_map/merge/pallas_call | solution.py:392
Async XLA Ops:
  0.6 15.2 %collective-permute-start = (bf16[1024,256]{1,0:T(8,128)(2,1)}, bf16[1024,256]{1,0:T(8,128)(2,1)S(1)}, u32[]{:S(2)}, u32[]{:S(2)}) collective-permute-start(bf16[1024,256]{1,0:T(8,128)(2,1)} %own_ref.1), channel_id=1, source_target_pairs={{0,96},{1,97},{2,98},{3,99},{4,100},{5,101},{6,102},{7,103},{8,104... | collective-permute-start | bytes 1572872 | tf_op jit(solution)/shard_map/ppermute | solution.py:54
  5.7 10.2 %copy-start = (bf16[1024,256]{1,0:T(8,128)(2,1)S(1)}, bf16[1024,256]{1,0:T(8,128)(2,1)}, u32[]{:S(2)}) copy-start(bf16[1024,256]{1,0:T(8,128)(2,1)} %own_ref.1) | copy-start | bytes 1572868
  5.7 24.2 %all-to-all-start = ((bf16[32,64,256]{2,1,0:T(8,128)(2,1)}), bf16[32,64,256]{2,1,0:T(8,128)(2,1)S(1)}, u32[]{:S(2)}, u32[]{:S(2)}) async-start(bf16[32,64,256]{2,1,0:T(8,128)(2,1)} %pack.1), calls=%async_computation | async-start | bytes 2097152 | tf_op jit(solution)/shard_map/all_to_all | solution.py:411
  16.5 2.0 %collective-permute-start.1 = (bf16[2,8,64,256]{3,2,1,0:T(8,128)(2,1)S(1)}, bf16[2,8,64,256]{3,2,1,0:T(8,128)(2,1)S(1)}, u32[]{:S(2)}, u32[]{:S(2)}) collective-permute-start(bf16[2,8,64,256]{3,2,1,0:T(8,128)(2,1)S(1)} %get-tuple-element.12), channel_id=1, source_target_pairs={{0,1},{1,0},{2,3},{3,2},{4,5},{5,4},{6,7},{7,6},{8,9},{9,8},{10,11... | collective-permute-start | bytes 1572872 | tf_op jit(solution)/shard_map/ppermute | solution.py:54
  29.9 2.7 %collective-permute-start.2 = (bf16[32,64,256]{2,1,0:T(8,128)(2,1)S(1)}, bf16[32,64,256]{2,1,0:T(8,128)(2,1)S(1)}, u32[]{:S(2)}, u32[]{:S(2)}) collective-permute-start(bf16[32,64,256]{2,1,0:T(8,128)(2,1)S(1)} %all-to-all-done.refs_2_), channel_id=1, source_target_pairs={{0,1},{1,0},{2,3},{3,2},{4,5},{5,4},{6,7},{7,6},{8,9},{9,8},{10,11... | collective-permute-start | bytes 3145736 | tf_op jit(solution)/shard_map/ppermute | solution.py:54

commit v8 on v7

--- a/solution.py
+++ b/solution.py
@@ -367,7 +367,8 @@
     )(place, *q_pieces, own, other)
 
 
-def merge_body(got_ref, mixed_ref, log_ref):
+def merge_body(got_ref, out_ref, log_ref, mixed_ref, left):
+    gives = []
     for block in range(2 * SIDES):
         sums = []
         for member in range(2):
@@ -385,6 +386,13 @@
                 mixed_ref[:, place * HD : (place + 1) * HD] = rows[head * 64 : (head + 1) * 64]
                 at = (pair * 2 + head) * 64
                 log_ref[place : place + 1, :] = joint[:, at : at + 64]
+        cols = slice(block * HELD * HD, (block + 1) * HELD * HD)
+        gives.append(
+            pltpu.make_async_copy(mixed_ref.at[:, cols], out_ref.at[:, cols], left.at[block])
+        )
+        gives[-1].start()
+    for give in gives:
+        give.wait()
 
 
 def merge(got):
@@ -396,7 +404,11 @@
             jax.ShapeDtypeStruct((HQ, 64), jnp.float32),
         ),
         in_specs=[whole],
-        out_specs=(whole, whole),
+        out_specs=(pl.BlockSpec(memory_space=pl.ANY), whole),
+        scratch_shapes=[
+            pltpu.VMEM((64, HQ * HD), jnp.bfloat16),
+            pltpu.SemaphoreType.DMA((2 * SIDES,)),
+        ],
         compiler_params=pltpu.CompilerParams(vmem_limit_bytes=8 * 2**20),
         name="merge",
     )(got.reshape(2, 2 * SIDES, DEPTH, 256))

time: 80 us -> 80.7 us (level)
  no operation moved by 1% of the time
where the time goes in v8:
time: 80.7 us; the launch traced here: 80.4 us
  Pallas kernels  27.1 us (34%)
  blocking collectives  24.3 us (30%)
  waiting for transfers between devices  16.3 us (20%)
  starting transfers between devices  11.8 us (15%)
  between operations  0.83 us (1%)
    all_to_all x1, blocking collectives, per_device(): got = lax.all_to_all(partial, EVERY, 0, 0, axis_index_groups=OUTPUT_GROUPS)  24.3 us
    pallas_call x1, Pallas kernels, attend(): pl.pallas_call(attend_body, out_shape=jax.ShapeDtypeStruct((16, DEPTH, 25...  21.7 us
    all_to_all x1, waiting for transfers between devices, per_device(): lax.all_to_all(pack(key_states, value_states), EVERY, 0, 0, axis_index_gr...  10.3 us
    all_to_all x1, starting transfers between devices, per_device(): lax.all_to_all(pack(key_states, value_states), EVERY, 0, 0, axis_index_gr...  8.6 us
    ppermute x3, waiting for transfers between devices, swapped(): return lax.ppermute(array, EVERY, [(i, i ^ bits) for i in range(DEVICES)])  6.03 us
    ppermute x3, starting transfers between devices, swapped(): return lax.ppermute(array, EVERY, [(i, i ^ bits) for i in range(DEVICES)])  3.18 us
    pallas_call x1, Pallas kernels, pack(): pl.pallas_call(pack_body, out_shape=jax.ShapeDtypeStruct((32, 64, 2 * HD)...  1.97 us
    pallas_call x1, Pallas kernels, merge(): pl.pallas_call(merge_body, out_shape=(jax.ShapeDtypeStruct((64, HQ * HD),...  1.71 us
  transfers between devices with their start and end apart: 4, of which 4 were waited for; matrix products, arithmetic and copies ran while one was open for 0% of the time, Pallas kernels for 5%

profile of v8, /device:TPU:2, one launch (start us, length us, event | category | flops | bytes accessed | tf_op | source)
XLA Modules:
  0.0 80.4 jit_solution(1900063299942337627)
XLA Ops:
  0.6 3.1 %collective-permute-start = (bf16[1024,256]{1,0:T(8,128)(2,1)}, bf16[1024,256]{1,0:T(8,128)(2,1)S(1)}, u32[]{:S(2)}, u32[]{:S(2)}) collective-permute-start(bf16[1024,256]{1,0:T(8,128)(2,1)} %own_ref.1), channel_id=1, source_target_pairs={{0,96},{1,97},{2,98},{3,99},{4,100},{5,101},{6,102},{7,103},{8,104... | collective-permute-start | bytes 1572872 | tf_op jit(solution)/shard_map/ppermute | solution.py:54
  3.7 2.0 %pack.1 = bf16[32,64,256]{2,1,0:T(8,128)(2,1)} custom-call(bf16[64,512]{1,0:T(8,128)(2,1)} %key_ref.1, bf16[64,512]{1,0:T(8,128)(2,1)} %value_ref.1), custom_call_target="tpu_custom_call" | custom-call | tf_op jit(solution)/shard_map/pack/pallas_call | solution.py:67
  5.7 0.0 copy-start
  5.7 8.6 %all-to-all-start = ((bf16[32,64,256]{2,1,0:T(8,128)(2,1)}), bf16[32,64,256]{2,1,0:T(8,128)(2,1)S(1)}, u32[]{:S(2)}, u32[]{:S(2)}) async-start(bf16[32,64,256]{2,1,0:T(8,128)(2,1)} %pack.1), calls=%async_computation | async-start | bytes 2097152 | tf_op jit(solution)/shard_map/all_to_all | solution.py:423
  14.3 0.1 pad_add_fusion.place
  14.4 1.5 %collective-permute-done.couple_ref = bf16[1024,256]{1,0:T(8,128)(2,1)S(1)} collective-permute-done((bf16[1024,256]{1,0:T(8,128)(2,1)}, bf16[1024,256]{1,0:T(8,128)(2,1)S(1)}, u32[]{:S(2)}, u32[]{:S(2)}) %collective-permute-start) | collective-permute-done | bytes 524320 | tf_op jit(solution)/shard_map/ppermute | solution.py:54
  15.9 0.0 copy-done
  15.9 0.6 split.1
  16.5 0.1 collective-permute-start.1
  16.6 1.9 %collective-permute-done.1.taken_ref = bf16[2,8,64,256]{3,2,1,0:T(8,128)(2,1)S(1)} collective-permute-done((bf16[2,8,64,256]{3,2,1,0:T(8,128)(2,1)S(1)}, bf16[2,8,64,256]{3,2,1,0:T(8,128)(2,1)S(1)}, u32[]{:S(2)}, u32[]{:S(2)}) %collective-permute-start.1) | collective-permute-done | bytes 524320 | tf_op jit(solution)/shard_map/ppermute | solution.py:54
  18.5 1.1 %arrange.1 = (bf16[2,2048,128]{2,1,0:T(8,128)(2,1)S(1)}, f32[2,4,8,512]{3,2,1,0:T(8,128)S(1)}) custom-call(s32[2]{0:T(128)S(1)} %pad_add_fusion.place, bf16[2,8,64,256]{3,2,1,0:T(8,128)(2,1)S(1)} %get-tuple-element.11.kept_ref, bf16[2,8,64,256]{3,2,1,0:T(8,128)(2,1)S(1)} %collective-permute-done.1.taken_ref), custom_call_target="tpu_custom_call" | custom-call | tf_op jit(solution)/shard_map/arrange/pallas_call | solution.py:144
  19.6 10.3 %all-to-all-done.refs_2_ = bf16[32,64,256]{2,1,0:T(8,128)(2,1)S(1)} async-done(((bf16[32,64,256]{2,1,0:T(8,128)(2,1)}), bf16[32,64,256]{2,1,0:T(8,128)(2,1)S(1)}, u32[]{:S(2)}, u32[]{:S(2)}) %all-to-all-start) | async-done | bytes 1048608 | tf_op jit(solution)/shard_map/all_to_all | solution.py:423
  29.9 0.0 collective-permute-start.2
  29.9 2.7 %collective-permute-done.2.refs_3_ = bf16[32,64,256]{2,1,0:T(8,128)(2,1)S(1)} collective-permute-done((bf16[32,64,256]{2,1,0:T(8,128)(2,1)S(1)}, bf16[32,64,256]{2,1,0:T(8,128)(2,1)S(1)}, u32[]{:S(2)}, u32[]{:S(2)}) %collective-permute-start.2) | collective-permute-done | bytes 1048608 | tf_op jit(solution)/shard_map/ppermute | solution.py:54
  32.5 21.7 %attend.1 = bf16[16,136,256]{2,1,0:T(8,128)(2,1)S(1)} custom-call(s32[2]{0:T(128)S(1)} %pad_add_fusion.place, bf16[2,2048,128]{2,1,0:T(8,128)(2,1)S(1)} %get-tuple-element.15.refs_0_, f32[2,4,8,512]{3,2,1,0:T(8,128)S(1)} %get-tuple-element.16.refs_1_, bf16[32,64,256]{2,1,0:T(8,128)(2,1)S(1)} %all-to-all-done.refs_2_, ...), custom_call_target="tpu_custom_call" | custom-call | flops 4831838208 | bytes 4194304 | tf_op jit(solution)/shard_map/attend/pallas_call | solution.py:346
  54.3 24.3 %all_to_all.10 = bf16[16,136,256]{2,1,0:T(8,128)(2,1)S(1)} all-to-all(bf16[16,136,256]{2,1,0:T(8,128)(2,1)S(1)} %attend.1), channel_id=1, replica_groups={{0,2,4,6,8,10,12,14,96,98,100,102,104,106,108,110},{1,3,5,7,9,11,13,15,..., dimensions={0} | all-to-all | bytes 2228224 | tf_op jit(solution)/shard_map/all_to_all | solution.py:434
  78.5 1.7 %merge.1 = (bf16[64,4096]{1,0:T(8,128)(2,1)}, f32[32,64]{1,0:T(8,128)}) custom-call(bf16[2,8,136,256]{3,2,1,0:T(8,128)(2,1)S(1)} %bitcast.4), custom_call_target="tpu_custom_call" | custom-call | tf_op jit(solution)/shard_map/merge/pallas_call | solution.py:400
Async XLA Ops:
  0.6 15.2 %collective-permute-start = (bf16[1024,256]{1,0:T(8,128)(2,1)}, bf16[1024,256]{1,0:T(8,128)(2,1)S(1)}, u32[]{:S(2)}, u32[]{:S(2)}) collective-permute-start(bf16[1024,256]{1,0:T(8,128)(2,1)} %own_ref.1), channel_id=1, source_target_pairs={{0,96},{1,97},{2,98},{3,99},{4,100},{5,101},{6,102},{7,103},{8,104... | collective-permute-start | bytes 1572872 | tf_op jit(solution)/shard_map/ppermute | solution.py:54
  5.7 10.2 %copy-start = (bf16[1024,256]{1,0:T(8,128)(2,1)S(1)}, bf16[1024,256]{1,0:T(8,128)(2,1)}, u32[]{:S(2)}) copy-start(bf16[1024,256]{1,0:T(8,128)(2,1)} %own_ref.1) | copy-start | bytes 1572868
  5.7 24.2 %all-to-all-start = ((bf16[32,64,256]{2,1,0:T(8,128)(2,1)}), bf16[32,64,256]{2,1,0:T(8,128)(2,1)S(1)}, u32[]{:S(2)}, u32[]{:S(2)}) async-start(bf16[32,64,256]{2,1,0:T(8,128)(2,1)} %pack.1), calls=%async_computation | async-start | bytes 2097152 | tf_op jit(solution)/shard_map/all_to_all | solution.py:423
  16.5 2.0 %collective-permute-start.1 = (bf16[2,8,64,256]{3,2,1,0:T(8,128)(2,1)S(1)}, bf16[2,8,64,256]{3,2,1,0:T(8,128)(2,1)S(1)}, u32[]{:S(2)}, u32[]{:S(2)}) collective-permute-start(bf16[2,8,64,256]{3,2,1,0:T(8,128)(2,1)S(1)} %get-tuple-element.12), channel_id=1, source_target_pairs={{0,1},{1,0},{2,3},{3,2},{4,5},{5,4},{6,7},{7,6},{8,9},{9,8},{10,11... | collective-permute-start | bytes 1572872 | tf_op jit(solution)/shard_map/ppermute | solution.py:54
  29.9 2.7 %collective-permute-start.2 = (bf16[32,64,256]{2,1,0:T(8,128)(2,1)S(1)}, bf16[32,64,256]{2,1,0:T(8,128)(2,1)S(1)}, u32[]{:S(2)}, u32[]{:S(2)}) collective-permute-start(bf16[32,64,256]{2,1,0:T(8,128)(2,1)S(1)} %all-to-all-done.refs_2_), channel_id=1, source_target_pairs={{0,1},{1,0},{2,3},{3,2},{4,5},{5,4},{6,7},{7,6},{8,9},{9,8},{10,11... | collective-permute-start | bytes 3145736 | tf_op jit(solution)/shard_map/ppermute | solution.py:54

commit v9 on v7

--- a/solution.py
+++ b/solution.py
@@ -214,9 +214,10 @@
         def ahead(tile):
             return score(q_all, tile, span, 256 if tile < 2 else 512)
 
-        ready = ahead(0)
-        for tile in range(4):
-            later = ahead(tile + 1) if tile < 3 else None
+        order = (3, 2, 1, 0)
+        ready = ahead(order[0])
+        for at, tile in enumerate(order):
+            later = ahead(order[at + 1]) if at < 3 else None
             edge, parts = ready[-256:], [ready[:256]] if tile >= 2 else []
             reach = in_row + (tile % 2) * 256 + core * 64 - half * 256
             keep = in_key <= reach

time: 80 us -> 79.9 us (level)
  Pallas kernels: 26.6 us -> 18.9 us
  blocking collectives: 24.3 us -> 31.8 us
    pallas_call x1, Pallas kernels: 21.7 us -> 14 us  [attend(): pl.pallas_call(attend_body, out_shape=jax.ShapeDtypeStruct((16, DEPTH, 25...]
    all_to_all x1, blocking collectives: 24.3 us -> 31.8 us  [per_device(): got = lax.all_to_all(partial, EVERY, 0, 0, axis_index_groups=OUTPUT_GROUPS)]
where the time goes in v9:
time: 79.9 us; the launch traced here: 79.5 us
  blocking collectives  31.8 us (40%)
  Pallas kernels  18.9 us (24%)
  waiting for transfers between devices  16.3 us (20%)
  starting transfers between devices  11.8 us (15%)
    all_to_all x1, blocking collectives, per_device(): got = lax.all_to_all(partial, EVERY, 0, 0, axis_index_groups=OUTPUT_GROUPS)  31.8 us
    pallas_call x1, Pallas kernels, attend(): pl.pallas_call(attend_body, out_shape=jax.ShapeDtypeStruct((16, DEPTH, 25...  14 us
    all_to_all x1, waiting for transfers between devices, per_device(): lax.all_to_all(pack(key_states, value_states), EVERY, 0, 0, axis_index_gr...  10.3 us
    all_to_all x1, starting transfers between devices, per_device(): lax.all_to_all(pack(key_states, value_states), EVERY, 0, 0, axis_index_gr...  8.6 us
    ppermute x3, waiting for transfers between devices, swapped(): return lax.ppermute(array, EVERY, [(i, i ^ bits) for i in range(DEVICES)])  6.03 us
    ppermute x3, starting transfers between devices, swapped(): return lax.ppermute(array, EVERY, [(i, i ^ bits) for i in range(DEVICES)])  3.18 us
    pallas_call x1, Pallas kernels, pack(): pl.pallas_call(pack_body, out_shape=jax.ShapeDtypeStruct((32, 64, 2 * HD)...  1.97 us
  transfers between devices with their start and end apart: 4, of which 4 were waited for; matrix products, arithmetic and copies ran while one was open for 0% of the time, Pallas kernels for 5%

profile of v9, /device:TPU:2, one launch (start us, length us, event | category | flops | bytes accessed | tf_op | source)
XLA Modules:
  0.0 79.5 jit_solution(17309828989202273281)
XLA Ops:
  0.6 3.1 %collective-permute-start = (bf16[1024,256]{1,0:T(8,128)(2,1)}, bf16[1024,256]{1,0:T(8,128)(2,1)S(1)}, u32[]{:S(2)}, u32[]{:S(2)}) collective-permute-start(bf16[1024,256]{1,0:T(8,128)(2,1)} %own_ref.1), channel_id=1, source_target_pairs={{0,96},{1,97},{2,98},{3,99},{4,100},{5,101},{6,102},{7,103},{8,104... | collective-permute-start | bytes 1572872 | tf_op jit(solution)/shard_map/ppermute | solution.py:54
  3.7 2.0 %pack.1 = bf16[32,64,256]{2,1,0:T(8,128)(2,1)} custom-call(bf16[64,512]{1,0:T(8,128)(2,1)} %key_ref.1, bf16[64,512]{1,0:T(8,128)(2,1)} %value_ref.1), custom_call_target="tpu_custom_call" | custom-call | tf_op jit(solution)/shard_map/pack/pallas_call | solution.py:67
  5.7 0.0 copy-start
  5.7 8.6 %all-to-all-start = ((bf16[32,64,256]{2,1,0:T(8,128)(2,1)}), bf16[32,64,256]{2,1,0:T(8,128)(2,1)S(1)}, u32[]{:S(2)}, u32[]{:S(2)}) async-start(bf16[32,64,256]{2,1,0:T(8,128)(2,1)} %pack.1), calls=%async_computation | async-start | bytes 2097152 | tf_op jit(solution)/shard_map/all_to_all | solution.py:412
  14.3 0.1 pad_add_fusion.place
  14.4 1.5 %collective-permute-done.couple_ref = bf16[1024,256]{1,0:T(8,128)(2,1)S(1)} collective-permute-done((bf16[1024,256]{1,0:T(8,128)(2,1)}, bf16[1024,256]{1,0:T(8,128)(2,1)S(1)}, u32[]{:S(2)}, u32[]{:S(2)}) %collective-permute-start) | collective-permute-done | bytes 524320 | tf_op jit(solution)/shard_map/ppermute | solution.py:54
  15.9 0.0 copy-done
  15.9 0.6 split.1
  16.5 0.1 collective-permute-start.1
  16.6 1.9 %collective-permute-done.1.taken_ref = bf16[2,8,64,256]{3,2,1,0:T(8,128)(2,1)S(1)} collective-permute-done((bf16[2,8,64,256]{3,2,1,0:T(8,128)(2,1)S(1)}, bf16[2,8,64,256]{3,2,1,0:T(8,128)(2,1)S(1)}, u32[]{:S(2)}, u32[]{:S(2)}) %collective-permute-start.1) | collective-permute-done | bytes 524320 | tf_op jit(solution)/shard_map/ppermute | solution.py:54
  18.5 1.1 %arrange.1 = (bf16[2,2048,128]{2,1,0:T(8,128)(2,1)S(1)}, f32[2,4,8,512]{3,2,1,0:T(8,128)S(1)}) custom-call(s32[2]{0:T(128)S(1)} %pad_add_fusion.place, bf16[2,8,64,256]{3,2,1,0:T(8,128)(2,1)S(1)} %get-tuple-element.11.kept_ref, bf16[2,8,64,256]{3,2,1,0:T(8,128)(2,1)S(1)} %collective-permute-done.1.taken_ref), custom_call_target="tpu_custom_call" | custom-call | tf_op jit(solution)/shard_map/arrange/pallas_call | solution.py:144
  19.6 10.3 %all-to-all-done.refs_2_ = bf16[32,64,256]{2,1,0:T(8,128)(2,1)S(1)} async-done(((bf16[32,64,256]{2,1,0:T(8,128)(2,1)}), bf16[32,64,256]{2,1,0:T(8,128)(2,1)S(1)}, u32[]{:S(2)}, u32[]{:S(2)}) %all-to-all-start) | async-done | bytes 1048608 | tf_op jit(solution)/shard_map/all_to_all | solution.py:412
  29.9 0.0 collective-permute-start.2
  29.9 2.7 %collective-permute-done.2.refs_3_ = bf16[32,64,256]{2,1,0:T(8,128)(2,1)S(1)} collective-permute-done((bf16[32,64,256]{2,1,0:T(8,128)(2,1)S(1)}, bf16[32,64,256]{2,1,0:T(8,128)(2,1)S(1)}, u32[]{:S(2)}, u32[]{:S(2)}) %collective-permute-start.2) | collective-permute-done | bytes 1048608 | tf_op jit(solution)/shard_map/ppermute | solution.py:54
  32.5 14.0 %attend.1 = bf16[16,136,256]{2,1,0:T(8,128)(2,1)S(1)} custom-call(s32[2]{0:T(128)S(1)} %pad_add_fusion.place, bf16[2,2048,128]{2,1,0:T(8,128)(2,1)S(1)} %get-tuple-element.15.refs_0_, f32[2,4,8,512]{3,2,1,0:T(8,128)S(1)} %get-tuple-element.16.refs_1_, bf16[32,64,256]{2,1,0:T(8,128)(2,1)S(1)} %all-to-all-done.refs_2_, ...), custom_call_target="tpu_custom_call" | custom-call | flops 4831838208 | bytes 4194304 | tf_op jit(solution)/shard_map/attend/pallas_call | solution.py:347
  46.6 31.8 %all_to_all.10 = bf16[16,136,256]{2,1,0:T(8,128)(2,1)S(1)} all-to-all(bf16[16,136,256]{2,1,0:T(8,128)(2,1)S(1)} %attend.1), channel_id=1, replica_groups={{0,2,4,6,8,10,12,14,96,98,100,102,104,106,108,110},{1,3,5,7,9,11,13,15,..., dimensions={0} | all-to-all | bytes 2228224 | tf_op jit(solution)/shard_map/all_to_all | solution.py:423
  78.4 1.2 %merge.1 = (bf16[64,4096]{1,0:T(8,128)(2,1)}, f32[32,64]{1,0:T(8,128)}) custom-call(bf16[2,8,136,256]{3,2,1,0:T(8,128)(2,1)S(1)} %bitcast.4), custom_call_target="tpu_custom_call" | custom-call | tf_op jit(solution)/shard_map/merge/pallas_call | solution.py:393
Async XLA Ops:
  0.6 15.2 %collective-permute-start = (bf16[1024,256]{1,0:T(8,128)(2,1)}, bf16[1024,256]{1,0:T(8,128)(2,1)S(1)}, u32[]{:S(2)}, u32[]{:S(2)}) collective-permute-start(bf16[1024,256]{1,0:T(8,128)(2,1)} %own_ref.1), channel_id=1, source_target_pairs={{0,96},{1,97},{2,98},{3,99},{4,100},{5,101},{6,102},{7,103},{8,104... | collective-permute-start | bytes 1572872 | tf_op jit(solution)/shard_map/ppermute | solution.py:54
  5.7 10.2 %copy-start = (bf16[1024,256]{1,0:T(8,128)(2,1)S(1)}, bf16[1024,256]{1,0:T(8,128)(2,1)}, u32[]{:S(2)}) copy-start(bf16[1024,256]{1,0:T(8,128)(2,1)} %own_ref.1) | copy-start | bytes 1572868
  5.7 24.2 %all-to-all-start = ((bf16[32,64,256]{2,1,0:T(8,128)(2,1)}), bf16[32,64,256]{2,1,0:T(8,128)(2,1)S(1)}, u32[]{:S(2)}, u32[]{:S(2)}) async-start(bf16[32,64,256]{2,1,0:T(8,128)(2,1)} %pack.1), calls=%async_computation | async-start | bytes 2097152 | tf_op jit(solution)/shard_map/all_to_all | solution.py:412
  16.5 2.0 %collective-permute-start.1 = (bf16[2,8,64,256]{3,2,1,0:T(8,128)(2,1)S(1)}, bf16[2,8,64,256]{3,2,1,0:T(8,128)(2,1)S(1)}, u32[]{:S(2)}, u32[]{:S(2)}) collective-permute-start(bf16[2,8,64,256]{3,2,1,0:T(8,128)(2,1)S(1)} %get-tuple-element.12), channel_id=1, source_target_pairs={{0,1},{1,0},{2,3},{3,2},{4,5},{5,4},{6,7},{7,6},{8,9},{9,8},{10,11... | collective-permute-start | bytes 1572872 | tf_op jit(solution)/shard_map/ppermute | solution.py:54
  29.9 2.7 %collective-permute-start.2 = (bf16[32,64,256]{2,1,0:T(8,128)(2,1)S(1)}, bf16[32,64,256]{2,1,0:T(8,128)(2,1)S(1)}, u32[]{:S(2)}, u32[]{:S(2)}) collective-permute-start(bf16[32,64,256]{2,1,0:T(8,128)(2,1)S(1)} %all-to-all-done.refs_2_), channel_id=1, source_target_pairs={{0,1},{1,0},{2,3},{3,2},{4,5},{5,4},{6,7},{7,6},{8,9},{9,8},{10,11... | collective-permute-start | bytes 3145736 | tf_op jit(solution)/shard_map/ppermute | solution.py:54
